TPU v7x, 256 devices: a whole 4x4x8 slice. The times are simulated.
256 devices in a mesh: dp: 4 (over y_hi, core), ctx: 64 (over z, y_lo, x).
Axes of the slice: x: 4, y: 4 (y_hi: 2, y_lo: 2; y = y_hi * 2 + y_lo), z: 8, core: 2. Of those that a mesh axis runs over, the one named last changes fastest.
Arguments:
- tokens: bfloat16 [4, 10240, 4096], P('dp', 'ctx'), may hold values from -6 to 6
- w_qkv: bfloat16 [4096, 5120], P('dp'), may hold values from -0.09375 to 0.09375
- col_scale: float32 [5120], replicated, may hold values from 0.4 to 1.6
- doc_ids: int32 [4, 10240], P('dp', 'ctx'), may hold values from 0 to 7, never falling along the last dimension, each value on 1 to 2560 neighbouring positions
Outputs:
- attended: bfloat16 [4, 10240, 4096], P('dp', 'ctx')
Inputs may be any that keep to these rules, and one draw needn't show every extreme that they name: `doc_ids`: along each sequence the ids never fall; every document holds at most 2560 tokens and some document holds exactly 2560.
All inputs are finite; a program needn't handle non-finite values.
Results may differ from a plain program's by a relative error of at most 0.04.
Values may be sent and summed in bfloat16 or wider, within the bound.
A program may use at most 192 MiB of HBM per device.

v0:
```python
import math

import jax
import jax.numpy as jnp
from jax import lax
from jax.sharding import PartitionSpec as P

QH = 32
KVH = 4
HD = 128


def shifted(block, axis, distance):
    devices = range(lax.axis_size(axis))
    route = [(i - distance, i) for i in devices if i - distance in devices]
    return lax.ppermute(block, axis, route)


def rotate(vectors, positions):
    half_width = vectors.shape[-1] // 2
    freqs = jnp.exp(
        -math.log(500000.0) * 2.0 * jnp.arange(half_width, dtype=jnp.float32) / vectors.shape[-1]
    )
    angles = positions.astype(jnp.float32)[:, None] * freqs[None, :]
    cosine = jnp.cos(angles)[:, None, :]
    sine = jnp.sin(angles)[:, None, :]
    first = vectors[..., :half_width]
    second = vectors[..., half_width:]
    return jnp.concatenate(
        [first * cosine - second * sine, second * cosine + first * sine], axis=-1
    )


def local(tokens, w_qkv, col_scale, doc_ids):
    tok_rows = tokens.shape[1]
    groups = QH // KVH
    score_scale = 1.0 / math.sqrt(HD)
    spread = lax.all_to_all(tokens, "dp", split_axis=2, concat_axis=0, tiled=True)
    summed = lax.psum_scatter(
        jnp.einsum("btd,dc->btc", spread, w_qkv, preferred_element_type=jnp.float32).astype(
            jnp.bfloat16
        ),
        "dp",
        scatter_dimension=0,
        tiled=True,
    ).astype(jnp.float32)
    qkv = summed[0] * col_scale
    base = lax.axis_index("ctx") * tok_rows
    positions = base + jnp.arange(tok_rows, dtype=jnp.int32)
    queries = rotate(qkv[:, : QH * HD].reshape(tok_rows, QH, HD), positions).astype(jnp.bfloat16)
    queries = queries.reshape(tok_rows, KVH, groups, HD)
    keys = rotate(qkv[:, QH * HD : (QH + KVH) * HD].reshape(tok_rows, KVH, HD), positions).astype(
        jnp.bfloat16
    )
    values = qkv[:, (QH + KVH) * HD :].reshape(tok_rows, KVH, HD).astype(jnp.bfloat16)
    query_docs = doc_ids[0]

    def attend(state, key_rows, value_rows, key_pos, key_docs):
        mask = (
            (key_docs[None, :] == query_docs[:, None])
            & (key_pos[None, :] <= positions[:, None])
            & (key_pos[None, :] >= 0)
        )
        run_max, run_sum, run_acc = state
        scores = (
            jnp.einsum("tgjd,sgd->gjts", queries, key_rows, preferred_element_type=jnp.float32)
            * score_scale
        )
        scores = jnp.where(mask[None, None], scores, -jnp.inf)
        new_max = jnp.maximum(run_max, jnp.max(scores, axis=-1))
        factor = jnp.exp(run_max - new_max)
        expo = jnp.exp(scores - new_max[..., None])
        new_sum = run_sum * factor + jnp.sum(expo, axis=-1)
        new_acc = run_acc * factor[..., None] + jnp.einsum(
            "gjts,sgd->gjtd",
            expo.astype(jnp.bfloat16),
            value_rows,
            preferred_element_type=jnp.float32,
        )
        return (new_max, new_sum, new_acc)

    state = (
        jnp.full((KVH, groups, tok_rows), -1e30, jnp.float32),
        jnp.zeros((KVH, groups, tok_rows), jnp.float32),
        jnp.zeros((KVH, groups, tok_rows, HD), jnp.float32),
    )
    state = attend(state, keys, values, positions, query_docs)
    span = min(16, lax.axis_size("ctx") // 2)

    def turn(step, carry):
        block, current = carry
        block = shifted((block[0], block[1], block[2]), "ctx", 1)
        key_pos = positions - (step + 1) * tok_rows
        current = attend(current, block[0], block[1], key_pos, block[2])
        return (block, current)

    final = lax.fori_loop(0, span, turn, ((keys, values, query_docs), state))
    state = final[1]
    run_max, run_sum, run_acc = state
    mixed = run_acc / run_sum[..., None]
    return mixed.transpose(2, 0, 1, 3).reshape(1, tok_rows, QH * HD).astype(jnp.bfloat16)


def solution(mesh):
    return jax.shard_map(
        local,
        mesh=mesh,
        in_specs=(P("dp", "ctx", None), P("dp", None), P(), P("dp", "ctx")),
        out_specs=P("dp", "ctx", None),
        check_vma=False,
    )
```

profile of v0, /device:TPU:72, one launch (start us, length us, event | category | flops | bytes accessed | tf_op | source)
XLA Modules:
  0.0 545.9 jit_solution(9981145204996563690)
XLA Ops:
  6.5 9.8 %copy.25 = bf16[1,160,4096]{1,0,2:T(2,128)(2,1)} copy(bf16[1,160,4096]{2,1,0:T(8,128)(2,1)} %param.6) | data formatting | bytes 2621440 | tf_op args[0]
  16.9 23.6 %reduce = bf16[4096,160]{1,0:T(8,128)(2,1)S(1)} reduce(bf16[4096,1,160]{2,1,0:T(2,128)(2,1)} %bitcast.91, bf16[]{:T(256)} %broadcast.243), dimensions={1}, to_apply=%bitcast.66.reduce_sub_computation | reduce | bytes 2621442
  43.7 22.1 %all_to_all.18 = bf16[4,2,81920]{2,1,0:T(2,128)(2,1)S(1)} all-to-all(bf16[4,2,81920]{2,1,0:T(2,128)(2,1)S(1)} %reshape.275), channel_id=1, replica_groups=mesh['dp'=4,'ctx'=64] {'dp'}, dimensions={0} | all-to-all | bytes 2621440 | tf_op jit(solution)/shard_map/all_to_all | solution.py:38
  65.9 4.5 reshape.276
  74.2 12.8 %fusion.20 = bf16[4,160,5120]{2,1,0:T(8,128)(2,1)} fusion(bf16[1024,5120]{1,0:T(8,128)(2,1)} %param.7, bf16[1,160,4,1024]{3,1,2,0:T(8,128)(2,1)S(1)} %copy.27), kind=kOutput, calls=%fused_computation.25 | convolution fusion | flops 6714163200 | bytes 18350080 | tf_op jit(solution)/shard_map/btd,dc->btc/dot_general | solution.py:40
  88.3 70.8 %reduce-scatter.2.cloned.1.call-done = bf16[1,160,5120]{2,1,0:T(8,128)(2,1)} async-done(((bf16[4,160,5120]{2,1,0:T(8,128)(2,1)}), bf16[1,160,5120]{2,1,0:T(8,128)(2,1)}) %reduce-scatter.2.cloned.1.call-update) | async-done | bytes 1638416 | tf_op jit(solution)/shard_map/reduce_scatter | solution.py:39
  174.0 362.3 %while.24 = (s32[]{:T(128)}, bf16[160,4,128]{2,0,1:T(8,128)(2,1)S(1)}, bf16[160,4,128]{2,0,1:T(8,128)(2,1)S(1)}, s32[160]{0:T(256)S(1)}, f32[4,8,160]{2,1,0:T(8,...) while((s32[]{:T(128)}, ...), condition=%wide.region_6.7_spmd.clone, body=%wide.region_3.6_spmd.clone.sunk | while | flops 429865760 | bytes 19116104 | solution.py:97
  184.2 6.5 %collective-permute-done = bf16[160,4,128]{2,0,1:T(8,128)(2,1)S(1)} collective-permute-done((bf16[160,4,128]{2,0,1:T(8,128)(2,1)S(1)}, bf16[160,4,128]{2,0,1:T(8,128)(2,1)S(1)}, u32[]{:S(2)}, u32[]{:S(2)}) %collective-permute-start) | collective-permute-done | bytes 163872 | tf_op jit(solution)/shard_map/while/body/eval_jaxpr/ppermute | solution.py:16
  206.3 5.6 %collective-permute-done = bf16[160,4,128]{2,0,1:T(8,128)(2,1)S(1)} collective-permute-done((bf16[160,4,128]{2,0,1:T(8,128)(2,1)S(1)}, bf16[160,4,128]{2,0,1:T(8,128)(2,1)S(1)}, u32[]{:S(2)}, u32[]{:S(2)}) %collective-permute-start) | collective-permute-done | bytes 163872 | tf_op jit(solution)/shard_map/while/body/eval_jaxpr/ppermute | solution.py:16
  222.0 4.4 collective-permute-start.1
  229.6 6.2 %collective-permute-done = bf16[160,4,128]{2,0,1:T(8,128)(2,1)S(1)} collective-permute-done((bf16[160,4,128]{2,0,1:T(8,128)(2,1)S(1)}, bf16[160,4,128]{2,0,1:T(8,128)(2,1)S(1)}, u32[]{:S(2)}, u32[]{:S(2)}) %collective-permute-start) | collective-permute-done | bytes 163872 | tf_op jit(solution)/shard_map/while/body/eval_jaxpr/ppermute | solution.py:16
  244.3 4.1 collective-permute-start.1
  250.9 6.9 %collective-permute-done = bf16[160,4,128]{2,0,1:T(8,128)(2,1)S(1)} collective-permute-done((bf16[160,4,128]{2,0,1:T(8,128)(2,1)S(1)}, bf16[160,4,128]{2,0,1:T(8,128)(2,1)S(1)}, u32[]{:S(2)}, u32[]{:S(2)}) %collective-permute-start) | collective-permute-done | bytes 163872 | tf_op jit(solution)/shard_map/while/body/eval_jaxpr/ppermute | solution.py:16
  272.2 7.0 %collective-permute-done = bf16[160,4,128]{2,0,1:T(8,128)(2,1)S(1)} collective-permute-done((bf16[160,4,128]{2,0,1:T(8,128)(2,1)S(1)}, bf16[160,4,128]{2,0,1:T(8,128)(2,1)S(1)}, u32[]{:S(2)}, u32[]{:S(2)}) %collective-permute-start) | collective-permute-done | bytes 163872 | tf_op jit(solution)/shard_map/while/body/eval_jaxpr/ppermute | solution.py:16
  295.0 5.6 %collective-permute-done = bf16[160,4,128]{2,0,1:T(8,128)(2,1)S(1)} collective-permute-done((bf16[160,4,128]{2,0,1:T(8,128)(2,1)S(1)}, bf16[160,4,128]{2,0,1:T(8,128)(2,1)S(1)}, u32[]{:S(2)}, u32[]{:S(2)}) %collective-permute-start) | collective-permute-done | bytes 163872 | tf_op jit(solution)/shard_map/while/body/eval_jaxpr/ppermute | solution.py:16
  307.3 4.4 collective-permute-start.2
  311.7 4.4 collective-permute-start.1
  318.2 7.2 %collective-permute-done = bf16[160,4,128]{2,0,1:T(8,128)(2,1)S(1)} collective-permute-done((bf16[160,4,128]{2,0,1:T(8,128)(2,1)S(1)}, bf16[160,4,128]{2,0,1:T(8,128)(2,1)S(1)}, u32[]{:S(2)}, u32[]{:S(2)}) %collective-permute-start) | collective-permute-done | bytes 163872 | tf_op jit(solution)/shard_map/while/body/eval_jaxpr/ppermute | solution.py:16
  334.9 4.4 collective-permute-start.1
  341.5 7.2 %collective-permute-done = bf16[160,4,128]{2,0,1:T(8,128)(2,1)S(1)} collective-permute-done((bf16[160,4,128]{2,0,1:T(8,128)(2,1)S(1)}, bf16[160,4,128]{2,0,1:T(8,128)(2,1)S(1)}, u32[]{:S(2)}, u32[]{:S(2)}) %collective-permute-start) | collective-permute-done | bytes 163872 | tf_op jit(solution)/shard_map/while/body/eval_jaxpr/ppermute | solution.py:16
  357.5 4.4 collective-permute-start.1
  364.0 7.2 %collective-permute-done = bf16[160,4,128]{2,0,1:T(8,128)(2,1)S(1)} collective-permute-done((bf16[160,4,128]{2,0,1:T(8,128)(2,1)S(1)}, bf16[160,4,128]{2,0,1:T(8,128)(2,1)S(1)}, u32[]{:S(2)}, u32[]{:S(2)}) %collective-permute-start) | collective-permute-done | bytes 163872 | tf_op jit(solution)/shard_map/while/body/eval_jaxpr/ppermute | solution.py:16
  386.0 7.2 %collective-permute-done = bf16[160,4,128]{2,0,1:T(8,128)(2,1)S(1)} collective-permute-done((bf16[160,4,128]{2,0,1:T(8,128)(2,1)S(1)}, bf16[160,4,128]{2,0,1:T(8,128)(2,1)S(1)}, u32[]{:S(2)}, u32[]{:S(2)}) %collective-permute-start) | collective-permute-done | bytes 163872 | tf_op jit(solution)/shard_map/while/body/eval_jaxpr/ppermute | solution.py:16
  401.8 4.0 collective-permute-start.1
  408.0 7.2 %collective-permute-done = bf16[160,4,128]{2,0,1:T(8,128)(2,1)S(1)} collective-permute-done((bf16[160,4,128]{2,0,1:T(8,128)(2,1)S(1)}, bf16[160,4,128]{2,0,1:T(8,128)(2,1)S(1)}, u32[]{:S(2)}, u32[]{:S(2)}) %collective-permute-start) | collective-permute-done | bytes 163872 | tf_op jit(solution)/shard_map/while/body/eval_jaxpr/ppermute | solution.py:16
  430.0 7.2 %collective-permute-done = bf16[160,4,128]{2,0,1:T(8,128)(2,1)S(1)} collective-permute-done((bf16[160,4,128]{2,0,1:T(8,128)(2,1)S(1)}, bf16[160,4,128]{2,0,1:T(8,128)(2,1)S(1)}, u32[]{:S(2)}, u32[]{:S(2)}) %collective-permute-start) | collective-permute-done | bytes 163872 | tf_op jit(solution)/shard_map/while/body/eval_jaxpr/ppermute | solution.py:16
  447.0 4.4 collective-permute-start.1
  453.5 7.7 %collective-permute-done = bf16[160,4,128]{2,0,1:T(8,128)(2,1)S(1)} collective-permute-done((bf16[160,4,128]{2,0,1:T(8,128)(2,1)S(1)}, bf16[160,4,128]{2,0,1:T(8,128)(2,1)S(1)}, u32[]{:S(2)}, u32[]{:S(2)}) %collective-permute-start) | collective-permute-done | bytes 163872 | tf_op jit(solution)/shard_map/while/body/eval_jaxpr/ppermute | solution.py:16
  475.6 7.3 %collective-permute-done = bf16[160,4,128]{2,0,1:T(8,128)(2,1)S(1)} collective-permute-done((bf16[160,4,128]{2,0,1:T(8,128)(2,1)S(1)}, bf16[160,4,128]{2,0,1:T(8,128)(2,1)S(1)}, u32[]{:S(2)}, u32[]{:S(2)}) %collective-permute-start) | collective-permute-done | bytes 163872 | tf_op jit(solution)/shard_map/while/body/eval_jaxpr/ppermute | solution.py:16
  497.6 7.8 %collective-permute-done = bf16[160,4,128]{2,0,1:T(8,128)(2,1)S(1)} collective-permute-done((bf16[160,4,128]{2,0,1:T(8,128)(2,1)S(1)}, bf16[160,4,128]{2,0,1:T(8,128)(2,1)S(1)}, u32[]{:S(2)}, u32[]{:S(2)}) %collective-permute-start) | collective-permute-done | bytes 163872 | tf_op jit(solution)/shard_map/while/body/eval_jaxpr/ppermute | solution.py:16
  515.9 4.4 collective-permute-start.1
  524.2 5.4 collective-permute-done
  (308 shorter events, 238.1 us)
Async XLA Ops:
  6.5 152.5 %reduce-scatter.2.cloned.1.call-start = ((), (), s32[]{:S(2)}) async-start(), calls=%async_computation.2 | async-start | bytes 8192000 | tf_op jit(solution)/shard_map/reduce_scatter | solution.py:39
  174.2 9.9 %collective-permute-start.2 = (s32[160]{0:T(256)S(1)}, s32[160]{0:T(256)S(1)}, u32[]{:S(2)}, u32[]{:S(2)}) collective-permute-start(s32[160]{0:T(256)S(1)} %get-tuple-element.358), channel_id=1, source_target_pairs={{0,1},{1,2},{2,3},{3,4},{4,5},{5,6},{6,7},{7,8},{8,9},{9,10},{10,1... | collective-permute-start | bytes 1928 | tf_op jit(solution)/shard_map/while/body/eval_jaxpr/ppermute | solution.py:16
  177.6 16.7 %collective-permute-start.1 = (bf16[160,4,128]{2,0,1:T(8,128)(2,1)S(1)}, bf16[160,4,128]{2,0,1:T(8,128)(2,1)S(1)}, u32[]{:S(2)}, u32[]{:S(2)}) collective-permute-start(bf16[160,4,128]{2,0,1:T(8,128)(2,1)S(1)} %get-tuple-element.357), channel_id=1, source_target_pairs={{0,1},{1,2},{2,3},{3,4},{4,5},{5,6},{6,7},{7,8},{8,9},{9,10},{10,1... | collective-permute-start | bytes 491528 | tf_op jit(solution)/shard_map/while/body/eval_jaxpr/ppermute | solution.py:16
  181.0 9.8 %collective-permute-start = (bf16[160,4,128]{2,0,1:T(8,128)(2,1)S(1)}, bf16[160,4,128]{2,0,1:T(8,128)(2,1)S(1)}, u32[]{:S(2)}, u32[]{:S(2)}) collective-permute-start(bf16[160,4,128]{2,0,1:T(8,128)(2,1)S(1)} %get-tuple-element.356), channel_id=1, source_target_pairs={{0,1},{1,2},{2,3},{3,4},{4,5},{5,6},{6,7},{7,8},{8,9},{9,10},{10,1... | collective-permute-start | bytes 491528 | tf_op jit(solution)/shard_map/while/body/eval_jaxpr/ppermute | solution.py:16
  199.4 16.1 %collective-permute-start.1 = (bf16[160,4,128]{2,0,1:T(8,128)(2,1)S(1)}, bf16[160,4,128]{2,0,1:T(8,128)(2,1)S(1)}, u32[]{:S(2)}, u32[]{:S(2)}) collective-permute-start(bf16[160,4,128]{2,0,1:T(8,128)(2,1)S(1)} %get-tuple-element.357), channel_id=1, source_target_pairs={{0,1},{1,2},{2,3},{3,4},{4,5},{5,6},{6,7},{7,8},{8,9},{9,10},{10,1... | collective-permute-start | bytes 491528 | tf_op jit(solution)/shard_map/while/body/eval_jaxpr/ppermute | solution.py:16
  202.3 9.6 %collective-permute-start = (bf16[160,4,128]{2,0,1:T(8,128)(2,1)S(1)}, bf16[160,4,128]{2,0,1:T(8,128)(2,1)S(1)}, u32[]{:S(2)}, u32[]{:S(2)}) collective-permute-start(bf16[160,4,128]{2,0,1:T(8,128)(2,1)S(1)} %get-tuple-element.356), channel_id=1, source_target_pairs={{0,1},{1,2},{2,3},{3,4},{4,5},{5,6},{6,7},{7,8},{8,9},{9,10},{10,1... | collective-permute-start | bytes 491528 | tf_op jit(solution)/shard_map/while/body/eval_jaxpr/ppermute | solution.py:16
  218.6 10.8 %collective-permute-start.2 = (s32[160]{0:T(256)S(1)}, s32[160]{0:T(256)S(1)}, u32[]{:S(2)}, u32[]{:S(2)}) collective-permute-start(s32[160]{0:T(256)S(1)} %get-tuple-element.358), channel_id=1, source_target_pairs={{0,1},{1,2},{2,3},{3,4},{4,5},{5,6},{6,7},{7,8},{8,9},{9,10},{10,1... | collective-permute-start | bytes 1928 | tf_op jit(solution)/shard_map/while/body/eval_jaxpr/ppermute | solution.py:16
  222.0 17.3 %collective-permute-start.1 = (bf16[160,4,128]{2,0,1:T(8,128)(2,1)S(1)}, bf16[160,4,128]{2,0,1:T(8,128)(2,1)S(1)}, u32[]{:S(2)}, u32[]{:S(2)}) collective-permute-start(bf16[160,4,128]{2,0,1:T(8,128)(2,1)S(1)} %get-tuple-element.357), channel_id=1, source_target_pairs={{0,1},{1,2},{2,3},{3,4},{4,5},{5,6},{6,7},{7,8},{8,9},{9,10},{10,1... | collective-permute-start | bytes 491528 | tf_op jit(solution)/shard_map/while/body/eval_jaxpr/ppermute | solution.py:16
  226.4 9.3 %collective-permute-start = (bf16[160,4,128]{2,0,1:T(8,128)(2,1)S(1)}, bf16[160,4,128]{2,0,1:T(8,128)(2,1)S(1)}, u32[]{:S(2)}, u32[]{:S(2)}) collective-permute-start(bf16[160,4,128]{2,0,1:T(8,128)(2,1)S(1)} %get-tuple-element.356), channel_id=1, source_target_pairs={{0,1},{1,2},{2,3},{3,4},{4,5},{5,6},{6,7},{7,8},{8,9},{9,10},{10,1... | collective-permute-start | bytes 491528 | tf_op jit(solution)/shard_map/while/body/eval_jaxpr/ppermute | solution.py:16
  244.3 17.0 %collective-permute-start.1 = (bf16[160,4,128]{2,0,1:T(8,128)(2,1)S(1)}, bf16[160,4,128]{2,0,1:T(8,128)(2,1)S(1)}, u32[]{:S(2)}, u32[]{:S(2)}) collective-permute-start(bf16[160,4,128]{2,0,1:T(8,128)(2,1)S(1)} %get-tuple-element.357), channel_id=1, source_target_pairs={{0,1},{1,2},{2,3},{3,4},{4,5},{5,6},{6,7},{7,8},{8,9},{9,10},{10,1... | collective-permute-start | bytes 491528 | tf_op jit(solution)/shard_map/while/body/eval_jaxpr/ppermute | solution.py:16
  248.5 9.3 %collective-permute-start = (bf16[160,4,128]{2,0,1:T(8,128)(2,1)S(1)}, bf16[160,4,128]{2,0,1:T(8,128)(2,1)S(1)}, u32[]{:S(2)}, u32[]{:S(2)}) collective-permute-start(bf16[160,4,128]{2,0,1:T(8,128)(2,1)S(1)} %get-tuple-element.356), channel_id=1, source_target_pairs={{0,1},{1,2},{2,3},{3,4},{4,5},{5,6},{6,7},{7,8},{8,9},{9,10},{10,1... | collective-permute-start | bytes 491528 | tf_op jit(solution)/shard_map/while/body/eval_jaxpr/ppermute | solution.py:16
  266.4 16.3 %collective-permute-start.1 = (bf16[160,4,128]{2,0,1:T(8,128)(2,1)S(1)}, bf16[160,4,128]{2,0,1:T(8,128)(2,1)S(1)}, u32[]{:S(2)}, u32[]{:S(2)}) collective-permute-start(bf16[160,4,128]{2,0,1:T(8,128)(2,1)S(1)} %get-tuple-element.357), channel_id=1, source_target_pairs={{0,1},{1,2},{2,3},{3,4},{4,5},{5,6},{6,7},{7,8},{8,9},{9,10},{10,1... | collective-permute-start | bytes 491528 | tf_op jit(solution)/shard_map/while/body/eval_jaxpr/ppermute | solution.py:16
  269.8 9.3 %collective-permute-start = (bf16[160,4,128]{2,0,1:T(8,128)(2,1)S(1)}, bf16[160,4,128]{2,0,1:T(8,128)(2,1)S(1)}, u32[]{:S(2)}, u32[]{:S(2)}) collective-permute-start(bf16[160,4,128]{2,0,1:T(8,128)(2,1)S(1)} %get-tuple-element.356), channel_id=1, source_target_pairs={{0,1},{1,2},{2,3},{3,4},{4,5},{5,6},{6,7},{7,8},{8,9},{9,10},{10,1... | collective-permute-start | bytes 491528 | tf_op jit(solution)/shard_map/while/body/eval_jaxpr/ppermute | solution.py:16
  287.8 16.4 %collective-permute-start.1 = (bf16[160,4,128]{2,0,1:T(8,128)(2,1)S(1)}, bf16[160,4,128]{2,0,1:T(8,128)(2,1)S(1)}, u32[]{:S(2)}, u32[]{:S(2)}) collective-permute-start(bf16[160,4,128]{2,0,1:T(8,128)(2,1)S(1)} %get-tuple-element.357), channel_id=1, source_target_pairs={{0,1},{1,2},{2,3},{3,4},{4,5},{5,6},{6,7},{7,8},{8,9},{9,10},{10,1... | collective-permute-start | bytes 491528 | tf_op jit(solution)/shard_map/while/body/eval_jaxpr/ppermute | solution.py:16
  307.3 10.8 %collective-permute-start.2 = (s32[160]{0:T(256)S(1)}, s32[160]{0:T(256)S(1)}, u32[]{:S(2)}, u32[]{:S(2)}) collective-permute-start(s32[160]{0:T(256)S(1)} %get-tuple-element.358), channel_id=1, source_target_pairs={{0,1},{1,2},{2,3},{3,4},{4,5},{5,6},{6,7},{7,8},{8,9},{9,10},{10,1... | collective-permute-start | bytes 1928 | tf_op jit(solution)/shard_map/while/body/eval_jaxpr/ppermute | solution.py:16
  311.7 17.3 %collective-permute-start.1 = (bf16[160,4,128]{2,0,1:T(8,128)(2,1)S(1)}, bf16[160,4,128]{2,0,1:T(8,128)(2,1)S(1)}, u32[]{:S(2)}, u32[]{:S(2)}) collective-permute-start(bf16[160,4,128]{2,0,1:T(8,128)(2,1)S(1)} %get-tuple-element.357), channel_id=1, source_target_pairs={{0,1},{1,2},{2,3},{3,4},{4,5},{5,6},{6,7},{7,8},{8,9},{9,10},{10,1... | collective-permute-start | bytes 491528 | tf_op jit(solution)/shard_map/while/body/eval_jaxpr/ppermute | solution.py:16
  334.9 17.3 %collective-permute-start.1 = (bf16[160,4,128]{2,0,1:T(8,128)(2,1)S(1)}, bf16[160,4,128]{2,0,1:T(8,128)(2,1)S(1)}, u32[]{:S(2)}, u32[]{:S(2)}) collective-permute-start(bf16[160,4,128]{2,0,1:T(8,128)(2,1)S(1)} %get-tuple-element.357), channel_id=1, source_target_pairs={{0,1},{1,2},{2,3},{3,4},{4,5},{5,6},{6,7},{7,8},{8,9},{9,10},{10,1... | collective-permute-start | bytes 491528 | tf_op jit(solution)/shard_map/while/body/eval_jaxpr/ppermute | solution.py:16
  357.5 17.3 %collective-permute-start.1 = (bf16[160,4,128]{2,0,1:T(8,128)(2,1)S(1)}, bf16[160,4,128]{2,0,1:T(8,128)(2,1)S(1)}, u32[]{:S(2)}, u32[]{:S(2)}) collective-permute-start(bf16[160,4,128]{2,0,1:T(8,128)(2,1)S(1)} %get-tuple-element.357), channel_id=1, source_target_pairs={{0,1},{1,2},{2,3},{3,4},{4,5},{5,6},{6,7},{7,8},{8,9},{9,10},{10,1... | collective-permute-start | bytes 491528 | tf_op jit(solution)/shard_map/while/body/eval_jaxpr/ppermute | solution.py:16
  379.9 16.9 %collective-permute-start.1 = (bf16[160,4,128]{2,0,1:T(8,128)(2,1)S(1)}, bf16[160,4,128]{2,0,1:T(8,128)(2,1)S(1)}, u32[]{:S(2)}, u32[]{:S(2)}) collective-permute-start(bf16[160,4,128]{2,0,1:T(8,128)(2,1)S(1)} %get-tuple-element.357), channel_id=1, source_target_pairs={{0,1},{1,2},{2,3},{3,4},{4,5},{5,6},{6,7},{7,8},{8,9},{9,10},{10,1... | collective-permute-start | bytes 491528 | tf_op jit(solution)/shard_map/while/body/eval_jaxpr/ppermute | solution.py:16
  401.8 16.9 %collective-permute-start.1 = (bf16[160,4,128]{2,0,1:T(8,128)(2,1)S(1)}, bf16[160,4,128]{2,0,1:T(8,128)(2,1)S(1)}, u32[]{:S(2)}, u32[]{:S(2)}) collective-permute-start(bf16[160,4,128]{2,0,1:T(8,128)(2,1)S(1)} %get-tuple-element.357), channel_id=1, source_target_pairs={{0,1},{1,2},{2,3},{3,4},{4,5},{5,6},{6,7},{7,8},{8,9},{9,10},{10,1... | collective-permute-start | bytes 491528 | tf_op jit(solution)/shard_map/while/body/eval_jaxpr/ppermute | solution.py:16
  405.9 9.3 %collective-permute-start = (bf16[160,4,128]{2,0,1:T(8,128)(2,1)S(1)}, bf16[160,4,128]{2,0,1:T(8,128)(2,1)S(1)}, u32[]{:S(2)}, u32[]{:S(2)}) collective-permute-start(bf16[160,4,128]{2,0,1:T(8,128)(2,1)S(1)} %get-tuple-element.356), channel_id=1, source_target_pairs={{0,1},{1,2},{2,3},{3,4},{4,5},{5,6},{6,7},{7,8},{8,9},{9,10},{10,1... | collective-permute-start | bytes 491528 | tf_op jit(solution)/shard_map/while/body/eval_jaxpr/ppermute | solution.py:16
  423.8 16.9 %collective-permute-start.1 = (bf16[160,4,128]{2,0,1:T(8,128)(2,1)S(1)}, bf16[160,4,128]{2,0,1:T(8,128)(2,1)S(1)}, u32[]{:S(2)}, u32[]{:S(2)}) collective-permute-start(bf16[160,4,128]{2,0,1:T(8,128)(2,1)S(1)} %get-tuple-element.357), channel_id=1, source_target_pairs={{0,1},{1,2},{2,3},{3,4},{4,5},{5,6},{6,7},{7,8},{8,9},{9,10},{10,1... | collective-permute-start | bytes 491528 | tf_op jit(solution)/shard_map/while/body/eval_jaxpr/ppermute | solution.py:16
  427.8 9.3 %collective-permute-start = (bf16[160,4,128]{2,0,1:T(8,128)(2,1)S(1)}, bf16[160,4,128]{2,0,1:T(8,128)(2,1)S(1)}, u32[]{:S(2)}, u32[]{:S(2)}) collective-permute-start(bf16[160,4,128]{2,0,1:T(8,128)(2,1)S(1)} %get-tuple-element.356), channel_id=1, source_target_pairs={{0,1},{1,2},{2,3},{3,4},{4,5},{5,6},{6,7},{7,8},{8,9},{9,10},{10,1... | collective-permute-start | bytes 491528 | tf_op jit(solution)/shard_map/while/body/eval_jaxpr/ppermute | solution.py:16
  443.8 9.5 %collective-permute-start.2 = (s32[160]{0:T(256)S(1)}, s32[160]{0:T(256)S(1)}, u32[]{:S(2)}, u32[]{:S(2)}) collective-permute-start(s32[160]{0:T(256)S(1)} %get-tuple-element.358), channel_id=1, source_target_pairs={{0,1},{1,2},{2,3},{3,4},{4,5},{5,6},{6,7},{7,8},{8,9},{9,10},{10,1... | collective-permute-start | bytes 1928 | tf_op jit(solution)/shard_map/while/body/eval_jaxpr/ppermute | solution.py:16
  447.0 17.8 %collective-permute-start.1 = (bf16[160,4,128]{2,0,1:T(8,128)(2,1)S(1)}, bf16[160,4,128]{2,0,1:T(8,128)(2,1)S(1)}, u32[]{:S(2)}, u32[]{:S(2)}) collective-permute-start(bf16[160,4,128]{2,0,1:T(8,128)(2,1)S(1)} %get-tuple-element.357), channel_id=1, source_target_pairs={{0,1},{1,2},{2,3},{3,4},{4,5},{5,6},{6,7},{7,8},{8,9},{9,10},{10,1... | collective-permute-start | bytes 491528 | tf_op jit(solution)/shard_map/while/body/eval_jaxpr/ppermute | solution.py:16
  451.4 9.9 %collective-permute-start = (bf16[160,4,128]{2,0,1:T(8,128)(2,1)S(1)}, bf16[160,4,128]{2,0,1:T(8,128)(2,1)S(1)}, u32[]{:S(2)}, u32[]{:S(2)}) collective-permute-start(bf16[160,4,128]{2,0,1:T(8,128)(2,1)S(1)} %get-tuple-element.356), channel_id=1, source_target_pairs={{0,1},{1,2},{2,3},{3,4},{4,5},{5,6},{6,7},{7,8},{8,9},{9,10},{10,1... | collective-permute-start | bytes 491528 | tf_op jit(solution)/shard_map/while/body/eval_jaxpr/ppermute | solution.py:16
  469.9 16.6 %collective-permute-start.1 = (bf16[160,4,128]{2,0,1:T(8,128)(2,1)S(1)}, bf16[160,4,128]{2,0,1:T(8,128)(2,1)S(1)}, u32[]{:S(2)}, u32[]{:S(2)}) collective-permute-start(bf16[160,4,128]{2,0,1:T(8,128)(2,1)S(1)} %get-tuple-element.357), channel_id=1, source_target_pairs={{0,1},{1,2},{2,3},{3,4},{4,5},{5,6},{6,7},{7,8},{8,9},{9,10},{10,1... | collective-permute-start | bytes 491528 | tf_op jit(solution)/shard_map/while/body/eval_jaxpr/ppermute | solution.py:16
  472.1 10.8 %collective-permute-start = (bf16[160,4,128]{2,0,1:T(8,128)(2,1)S(1)}, bf16[160,4,128]{2,0,1:T(8,128)(2,1)S(1)}, u32[]{:S(2)}, u32[]{:S(2)}) collective-permute-start(bf16[160,4,128]{2,0,1:T(8,128)(2,1)S(1)} %get-tuple-element.356), channel_id=1, source_target_pairs={{0,1},{1,2},{2,3},{3,4},{4,5},{5,6},{6,7},{7,8},{8,9},{9,10},{10,1... | collective-permute-start | bytes 491528 | tf_op jit(solution)/shard_map/while/body/eval_jaxpr/ppermute | solution.py:16
  491.5 17.5 %collective-permute-start.1 = (bf16[160,4,128]{2,0,1:T(8,128)(2,1)S(1)}, bf16[160,4,128]{2,0,1:T(8,128)(2,1)S(1)}, u32[]{:S(2)}, u32[]{:S(2)}) collective-permute-start(bf16[160,4,128]{2,0,1:T(8,128)(2,1)S(1)} %get-tuple-element.357), channel_id=1, source_target_pairs={{0,1},{1,2},{2,3},{3,4},{4,5},{5,6},{6,7},{7,8},{8,9},{9,10},{10,1... | collective-permute-start | bytes 491528 | tf_op jit(solution)/shard_map/while/body/eval_jaxpr/ppermute | solution.py:16
  494.5 11.0 %collective-permute-start = (bf16[160,4,128]{2,0,1:T(8,128)(2,1)S(1)}, bf16[160,4,128]{2,0,1:T(8,128)(2,1)S(1)}, u32[]{:S(2)}, u32[]{:S(2)}) collective-permute-start(bf16[160,4,128]{2,0,1:T(8,128)(2,1)S(1)} %get-tuple-element.356), channel_id=1, source_target_pairs={{0,1},{1,2},{2,3},{3,4},{4,5},{5,6},{6,7},{7,8},{8,9},{9,10},{10,1... | collective-permute-start | bytes 491528 | tf_op jit(solution)/shard_map/while/body/eval_jaxpr/ppermute | solution.py:16
  512.2 11.8 %collective-permute-start.2 = (s32[160]{0:T(256)S(1)}, s32[160]{0:T(256)S(1)}, u32[]{:S(2)}, u32[]{:S(2)}) collective-permute-start(s32[160]{0:T(256)S(1)} %get-tuple-element.358), channel_id=1, source_target_pairs={{0,1},{1,2},{2,3},{3,4},{4,5},{5,6},{6,7},{7,8},{8,9},{9,10},{10,1... | collective-permute-start | bytes 1928 | tf_op jit(solution)/shard_map/while/body/eval_jaxpr/ppermute | solution.py:16
  515.9 17.3 %collective-permute-start.1 = (bf16[160,4,128]{2,0,1:T(8,128)(2,1)S(1)}, bf16[160,4,128]{2,0,1:T(8,128)(2,1)S(1)}, u32[]{:S(2)}, u32[]{:S(2)}) collective-permute-start(bf16[160,4,128]{2,0,1:T(8,128)(2,1)S(1)} %get-tuple-element.357), channel_id=1, source_target_pairs={{0,1},{1,2},{2,3},{3,4},{4,5},{5,6},{6,7},{7,8},{8,9},{9,10},{10,1... | collective-permute-start | bytes 491528 | tf_op jit(solution)/shard_map/while/body/eval_jaxpr/ppermute | solution.py:16
  (22 other events, 223.7 us)
Sparse Core Ops, SparseCore 0:
  87.2 71.8 reduce-scatter.1
where the time goes:
time: 548 us; the launch traced here: 546 us
  waiting for transfers between devices  182 us (33%)
  starting transfers between devices  141 us (26%)
  matrix products  101 us (18%)
  other arithmetic  52.6 us (10%)
  local copies, waits for them, and re-layouts  31.8 us (6%)
  blocking collectives  22.1 us (4%)
  between operations  13.6 us (2%)
    ppermute x48, starting transfers between devices, shifted(): return lax.ppermute(block, axis, route)  141 us
    ppermute x48, waiting for transfers between devices, shifted(): return lax.ppermute(block, axis, route)  111 us
    reduce_scatter x1, waiting for transfers between devices, local(): lax.psum_scatter(jnp.einsum('btd,dc->btc', spread, w_qkv, preferred_eleme...  70.8 us
    dot_general x17, matrix products, attend(): jnp.einsum('gjts,sgd->gjtd', expo.astype(jnp.bfloat16), value_rows, prefe...  51.1 us
    dot_general x17, matrix products, attend(): jnp.einsum('tgjd,sgd->gjts', queries, key_rows, preferred_element_type=jn...  36.8 us
    unnamed x19, local copies, waits for them, and re-layouts  25.9 us
    unnamed x1, other arithmetic  23.6 us
    all_to_all x1, blocking collectives, local(): lax.all_to_all(tokens, 'dp', split_axis=2, concat_axis=0, tiled=True)  22.1 us
  transfers between devices with their start and end apart: 49, of which 19 were waited for; matrix products, arithmetic and copies ran while one was open for 11% of the time, Pallas kernels for 0%

commit v1 on v0

v1 whole, which is shorter than its diff:
```python
import math

import jax
import jax.numpy as jnp
from jax import lax
from jax.experimental import pallas as pl
from jax.experimental.pallas import tpu as pltpu
from jax.sharding import PartitionSpec as P

MESH = pl.DeviceIdType.MESH
QH = 32
KVH = 4
HD = 128
T = 160
SLICE = 1024
CH = 512
NCH = 10
SPAN = 16
BLK = 2 * T + 16
F32 = jnp.float32
BF16 = jnp.bfloat16


def project_kernel(
    tok, w, scale, cosf, sinf, docs,
    q_out, kv,
    wv, xo, xp, po, p1, sso, rso, ssp, rsp, sx, rx, own,
    w_sem, loc_sem, tok_s, tok_r, sso_s, sso_r, ssp_s, ssp_r, sx_s, sx_r, h_s, h_r, h_r2,
):
    dp = lax.axis_index("dp")
    ctx = lax.axis_index("ctx")
    h = dp // 2
    k = dp % 2
    z = ctx // 8
    b = (ctx // 4) % 2
    x = ctx % 4

    def place(h_, k_, z_, b_, x_):
        return (h_ * 2 + k_, z_ * 8 + b_ * 4 + x_)

    sib = place(h, 1 - k, z, b, x)
    par = place(1 - h, k, z, 1 - b, x)
    parx = place(1 - h, 1 - k, z, 1 - b, x)
    z_up = place(h, k, (z + 1) % 8, b, x)
    z_dn = place(h, k, (z + 7) % 8, b, x)
    xi, xm, x2 = (x + 1) % 4, (x + 3) % 4, (x + 2) % 4
    d_i = place(h, k, z, b, xi)
    d_m = place(h, k, z, b, xm)
    d_2 = place(h, k, z, b, x2)
    d_y = place(h, k, z, 1 - b, x)

    def cols(i):
        return pl.ds(pl.multiple_of(((i + 8) % 10) * CH, CH), CH)

    def tok_cols(j):
        return pl.ds(pl.multiple_of(j * SLICE, SLICE), SLICE)

    def w_copy(i):
        return pltpu.make_async_copy(w.at[:, cols(i)], wv.at[i], w_sem.at[i])

    own_tok = pltpu.make_async_copy(tok.at[:, tok_cols(2 * h + k)], xo.at[pl.ds(0, T)], loc_sem.at[0])
    own_tok.start()
    for i in range(NCH):
        w_copy(i).start()

    bar = pltpu.get_barrier_semaphore()
    for dev in (sib, par, parx, z_dn, d_i, d_m, d_2, d_y):
        pl.semaphore_signal(bar, inc=1, device_id=dev, device_id_type=MESH)
    pl.semaphore_wait(bar, 8)

    def remote(src, dst, s, r, dev):
        return pltpu.make_async_remote_copy(
            src_ref=src, dst_ref=dst, send_sem=s, recv_sem=r, device_id=dev, device_id_type=MESH
        )

    t_par = remote(tok.at[:, tok_cols(2 * (1 - h) + k)], xp.at[pl.ds(0, T)], tok_s.at[0], tok_r.at[0], par)
    t_parx = remote(tok.at[:, tok_cols(2 * (1 - h) + 1 - k)], xp.at[pl.ds(T, T)], tok_s.at[1], tok_r.at[1], parx)
    t_sib = remote(tok.at[:, tok_cols(2 * h + 1 - k)], xo.at[pl.ds(T, T)], tok_s.at[2], tok_r.at[2], sib)
    t_par.start()
    t_parx.start()
    t_sib.start()

    own_tok.wait()
    t_sib.wait_recv()

    def sso_copy(i):
        return remote(sso.at[i], rso.at[i], sso_s.at[i], sso_r.at[i], sib)

    def ssp_copy(i):
        return remote(ssp.at[i], rsp.at[i], ssp_s.at[i], ssp_r.at[i], sib)

    def sx_copy(i):
        return remote(sx.at[i], rx.at[i], sx_s.at[i], sx_r.at[i], par)

    def own_part(i, c):
        w_copy(i).wait()
        part = jnp.dot(xo[...], wv[i], preferred_element_type=F32)
        po[i] = part[:T]
        sso[i] = part[T:].astype(BF16)
        sso_copy(i).start()
        return c

    lax.fori_loop(0, NCH, own_part, 0)

    t_par.wait_recv()
    t_parx.wait_recv()

    def partner_part(i, c):
        @pl.when(i < NCH)
        def _():
            part = jnp.dot(xp[...], wv[i], preferred_element_type=F32)
            p1[i] = part[:T].astype(BF16)
            ssp[i] = part[T:].astype(BF16)
            ssp_copy(i).start()

        @pl.when(i > 0)
        def _():
            ssp_copy(i - 1).wait_recv()
            sx[i - 1] = (p1[i - 1].astype(F32) + rsp[i - 1].astype(F32)).astype(BF16)
            sx_copy(i - 1).start()

        return c

    lax.fori_loop(0, NCH + 1, partner_part, 0)

    def summed(i):
        sso_copy(i).wait_recv()
        sx_copy(i).wait_recv()
        return (po[i] + rso[i].astype(F32) + rx[i].astype(F32)) * scale[(i + 8) % 10]

    def turned(u):
        return u * cosf[...] + pltpu.roll(u, HD // 2, 1) * sinf[...]

    own[pl.ds(2 * T, 16), :] = jnp.zeros((16, CH), BF16)
    own[pl.ds(2 * T, 16), pl.ds(0, T)] = jnp.broadcast_to(docs[...].astype(F32), (16, T)).astype(BF16)
    u = summed(0)
    for g in range(KVH):
        own[pl.ds(0, T), g * HD:(g + 1) * HD] = turned(u[:, g * HD:(g + 1) * HD]).astype(BF16)
    own[pl.ds(T, T), :] = summed(1).astype(BF16)

    put_own = pltpu.make_async_copy(own, kv.at[SPAN], loc_sem.at[1])
    put_own.start()

    K_ROWS = (0, T)
    V_ROWS = (T, T + 16)
    ALL = (0, BLK)

    def send(n, src, o, dist, dev, rows=ALL, sem=None):
        sem = h_r if sem is None else sem
        at = pl.ds(rows[0], rows[1])
        src = own if src else kv.at[SPAN - o]
        return remote(src.at[at], kv.at[SPAN - o - dist, at], h_s.at[n], sem.at[SPAN - o - dist], dev)

    def arrive(o, rows=ALL, sem=None):
        sem = h_r if sem is None else sem
        at = pl.ds(rows[0], rows[1])
        remote(kv.at[SPAN - o, at], kv.at[SPAN - o, at], h_s.at[0], sem.at[SPAN - o], sib).wait_recv()

    def late(v):
        return v < x

    ydist = 4 - 8 * b

    def y_first(n):
        return send(n, True, 0, ydist, d_y)

    def y_last(n):
        return send(n, False, 16, ydist, d_y)

    row = ((3, xi, d_i), (4, xm, d_m), (5, x2, d_2))

    z1 = send(0, True, 0, 8, z_up)
    z1.start()

    @pl.when(b == 0)
    def _():
        y_first(2).start()

    for n, v, dev in row:
        @pl.when(v > x)
        def _():
            send(n, True, 0, v - x, dev).start()

    def finish_q(i, c):
        u = summed(i)
        for g in range(CH // HD):
            at = pl.multiple_of((i - 2) * CH + g * HD, HD)
            q_out[:, pl.ds(at, HD)] = turned(u[:, g * HD:(g + 1) * HD]).astype(BF16)
        return c

    def finish(lo, hi):
        lax.fori_loop(lo, hi, finish_q, 0)

    finish(2, 4)
    arrive(8)
    z2 = send(1, False, 8, 8, z_up)
    a_i = send(6, False, 8, xi - x, d_i)
    a_m = send(7, False, 8, xm - x, d_m)
    a_y = send(8, False, 8, ydist, d_y)
    z2.start()
    a_i.start()
    a_m.start()
    a_y.start()

    yo = jnp.where(b == 1, 4, 12)

    def spread_start():
        arrive(yo)
        send(14, False, yo, xi - x, d_i).start()
        send(15, False, yo, xm - x, d_m).start()

    def spread_on():
        arrive(yo + x - xm)
        send(16, False, yo + x - xm, xi - x, d_i, K_ROWS).start()
        arrive(yo + x - xi)
        send(17, False, yo + x - xi, xm - x, d_m, V_ROWS, h_r2).start()

    finish(4, 5)

    @pl.when(b == 1)
    def _():
        spread_start()

    arrive(8 + x - xm)
    fa_i = send(9, False, 8 + x - xm, xi - x, d_i, K_ROWS)
    fa_y1 = send(10, False, 8 + x - xm, ydist, d_y)
    fa_i.start()
    fa_y1.start()
    arrive(8 + x - xi)
    fa_m = send(11, False, 8 + x - xi, xm - x, d_m, V_ROWS, h_r2)
    fa_y2 = send(12, False, 8 + x - xi, ydist, d_y)
    fa_m.start()
    fa_y2.start()
    finish(5, 6)

    arrive(16)
    for n, v, dev in row:
        @pl.when(v < x)
        def _():
            send(n, False, 16, v - x, dev).start()

    @pl.when(b == 1)
    def _():
        y_last(2).start()

    arrive(8 + x - x2, K_ROWS)
    arrive(8 + x - x2, V_ROWS, h_r2)
    fa_y3 = send(13, False, 8 + x - x2, ydist, d_y)
    fa_y3.start()

    @pl.when(b == 1)
    def _():
        spread_on()

    finish(6, 8)

    @pl.when(b == 0)
    def _():
        spread_start()

    finish(8, 9)

    @pl.when(b == 0)
    def _():
        spread_on()

    finish(9, 10)

    arrive(yo + x - x2, K_ROWS)
    arrive(yo + x - x2, V_ROWS, h_r2)
    for v in (xi, xm, x2):
        d = x - v
        arrive(jnp.where(d > 0, d, 16 + d))
    for v in (x, xi, xm, x2):
        arrive(8 - ydist + x - v)

    put_own.wait()
    t_par.wait_send()
    t_parx.wait_send()
    t_sib.wait_send()

    def sent(i, c):
        sso_copy(i).wait_send()
        ssp_copy(i).wait_send()
        sx_copy(i).wait_send()
        return c

    lax.fori_loop(0, NCH, sent, 0)
    for n in (0, 1, 2, 3, 4, 5, 6, 7, 8, 10, 12, 13, 14, 15):
        send(n, True, 0, 8, z_up).wait_send()
    for n in (9, 16):
        send(n, True, 0, 8, z_up, K_ROWS).wait_send()
    for n in (11, 17):
        send(n, True, 0, 8, z_up, V_ROWS).wait_send()


def project(tok, w, scale, cosf, sinf, docs):
    vmem = pl.BlockSpec(memory_space=pltpu.VMEM)
    hbm = pl.BlockSpec(memory_space=pl.ANY)
    chunks = pltpu.VMEM((NCH, T, CH), BF16)
    dma = pltpu.SemaphoreType.DMA
    return pl.pallas_call(
        project_kernel,
        out_shape=(
            jax.ShapeDtypeStruct((T, QH * HD), BF16),
            jax.ShapeDtypeStruct((SPAN + 1, BLK, CH), BF16),
        ),
        in_specs=[hbm, hbm, vmem, vmem, vmem, vmem],
        out_specs=(vmem, hbm),
        scratch_shapes=[
            pltpu.VMEM((NCH, SLICE, CH), BF16),
            pltpu.VMEM((2 * T, SLICE), BF16),
            pltpu.VMEM((2 * T, SLICE), BF16),
            pltpu.VMEM((NCH, T, CH), F32),
            chunks, chunks, chunks, chunks, chunks, chunks, chunks,
            pltpu.VMEM((BLK, CH), BF16),
            dma((NCH,)), dma((2,)), dma((3,)), dma((3,)),
            dma((NCH,)), dma((NCH,)), dma((NCH,)), dma((NCH,)), dma((NCH,)), dma((NCH,)),
            dma((18,)), dma((SPAN + 1,)), dma((SPAN + 1,)),
        ],
        compiler_params=pltpu.CompilerParams(
            collective_id=0, has_side_effects=True, vmem_limit_bytes=56 << 20
        ),
        name="project",
    )(tok, w, scale, cosf, sinf, docs)


def attend_kernel(q, kv, docs, out, keys, values, key_docs, bias, sem):
    k_copy = pltpu.make_async_copy(kv.at[:, pl.ds(0, T)], keys, sem.at[0])
    v_copy = pltpu.make_async_copy(kv.at[:, pl.ds(T, T)], values, sem.at[1])
    d_copy = pltpu.make_async_copy(kv.at[:, pl.ds(2 * T, 16)], key_docs, sem.at[2])
    d_copy.start()
    k_copy.start()
    v_copy.start()
    n_keys = (SPAN + 1) * T
    ctx = lax.axis_index("ctx")
    mine = docs[...].astype(F32)
    d_copy.wait()
    start = jnp.zeros((T, 1), F32)
    for i in range(SPAN + 1):
        theirs = key_docs[i, 0:1, 0:T].astype(F32)
        if i == SPAN:
            start += jnp.sum((theirs < mine).astype(F32), axis=1, keepdims=True)
        else:
            valid = (ctx >= SPAN - i).astype(F32)
            start -= valid * jnp.sum((theirs == mine).astype(F32), axis=1, keepdims=True)
    at = lax.broadcasted_iota(jnp.int32, (T, n_keys), 1).astype(F32) - float(SPAN * T)
    t = lax.broadcasted_iota(jnp.int32, (T, n_keys), 0).astype(F32)
    bias[...] = jnp.where((at >= start) & (at <= t), 0.0, -jnp.inf)
    k_copy.wait()
    v_copy.wait()
    factor = math.log2(math.e) / math.sqrt(HD)
    group = QH // KVH

    for g in range(KVH):
        kg = keys[:, :, g * HD:(g + 1) * HD].reshape(n_keys, HD)
        vg = values[:, :, g * HD:(g + 1) * HD].reshape(n_keys, HD)

        def head(j, c):
            cols = pl.ds(pl.multiple_of((g * group + j) * HD, HD), HD)
            s = lax.dot_general(q[:, cols], kg, (((1,), (1,)), ((), ())), preferred_element_type=F32)
            s = s + bias[...]
            m = jnp.max(s, axis=1, keepdims=True)
            p = jnp.exp2((s - m) * factor)
            total = jnp.sum(p, axis=1, keepdims=True)
            o = jnp.dot(p.astype(BF16), vg, preferred_element_type=F32)
            out[:, cols] = (o / total).astype(BF16)
            return c

        lax.fori_loop(0, group, head, 0)


def attend(q, kv, docs):
    vmem = pl.BlockSpec(memory_space=pltpu.VMEM)
    n = SPAN + 1
    return pl.pallas_call(
        attend_kernel,
        out_shape=jax.ShapeDtypeStruct((T, QH * HD), BF16),
        in_specs=[vmem, pl.BlockSpec(memory_space=pl.ANY), vmem],
        out_specs=vmem,
        scratch_shapes=[
            pltpu.VMEM((n, T, CH), BF16),
            pltpu.VMEM((n, T, CH), BF16),
            pltpu.VMEM((n, 16, CH), BF16),
            pltpu.VMEM((T, n * T), F32),
            pltpu.SemaphoreType.DMA((3,)),
        ],
        compiler_params=pltpu.CompilerParams(vmem_limit_bytes=56 << 20),
        name="attend",
    )(q, kv, docs)


def local(tokens, w_qkv, col_scale, doc_ids):
    positions = lax.axis_index("ctx") * T + jnp.arange(T, dtype=jnp.int32)
    half = HD // 2
    freqs = jnp.exp(-math.log(500000.0) * 2.0 * jnp.arange(half, dtype=F32) / HD)
    angles = positions.astype(F32)[:, None] * freqs[None, :]
    cosine, sine = jnp.cos(angles), jnp.sin(angles)
    cosf = jnp.concatenate([cosine, cosine], axis=1)
    sinf = jnp.concatenate([-sine, sine], axis=1)
    q, kv = project(
        tokens[0], w_qkv, col_scale.reshape(NCH, 1, CH), cosf, sinf, doc_ids
    )
    out = attend(q, kv, doc_ids.reshape(T, 1))
    return out[None]


def solution(mesh):
    return jax.shard_map(
        local,
        mesh=mesh,
        in_specs=(P("dp", "ctx", None), P("dp", None), P(), P("dp", "ctx")),
        out_specs=P("dp", "ctx", None),
        check_vma=False,
    )
```

time: 548 us -> 139 us (0.25)
  the two profiles are of different devices: /device:TPU:72 before, /device:TPU:16 now
where the time goes in v1:
time: 139 us
  Pallas kernels  136 us (98%)
  local copies, waits for them, and re-layouts  1.43 us (1%)
    pallas_call x1, Pallas kernels, project(): pl.pallas_call(project_kernel, out_shape=(jax.ShapeDtypeStruct((T, QH * H...  95 us
    pallas_call x1, Pallas kernels, attend(): pl.pallas_call(attend_kernel, out_shape=jax.ShapeDtypeStruct((T, QH * HD)...  41.2 us

profile of v1, /device:TPU:16, one launch (start us, length us, event | category | flops | bytes accessed | tf_op | source)
XLA Modules:
  0.0 138.8 jit_solution(17557452429539269010)
XLA Ops:
  0.0 1.4 %copy.5.docs = s32[160,1]{1,0:T(8,128)} copy(s32[160,1]{0,1:T(1,128)} %bitcast.6) | data formatting | bytes 1280 | tf_op jit(solution)/shard_map/reshape | solution.py:404
  1.4 0.4 fusion
  1.8 0.8 pad_maximum_fusion
  2.6 95.0 %project.1 = (bf16[160,4096]{1,0:T(8,128)(2,1)}, bf16[17,336,512]{2,1,0:T(8,128)(2,1)}) custom-call(bf16[160,4096]{1,0:T(8,128)(2,1)} %bitcast.4, bf16[1024,5120]{1,0:T(8,128)(2,1)} %w.1, f32[10,1,512]{2,1,0:T(1,128)} %bitcast.5, f32[160,128]{1,0:T(8,128)} %get-tuple-element.12.cosf, f32[160,128]{1,0:T(8,128)} %get-tuple-element.13.sinf, s32[1,160]{1,0:T(1,128)} %docs.1), custom_call_target="tpu_custom_call" | custom-call | tf_op jit(solution)/shard_map/project/pallas_call | solution.py:302
  97.6 41.2 %attend.1 = bf16[160,4096]{1,0:T(8,128)(2,1)} custom-call(bf16[160,4096]{1,0:T(8,128)(2,1)} %get-tuple-element.7.q, bf16[17,336,512]{2,1,0:T(8,128)(2,1)} %get-tuple-element.8.kv, s32[160,1]{1,0:T(8,128)} %copy.5.docs), custom_call_target="tpu_custom_call" | custom-call | tf_op jit(solution)/shard_map/attend/pallas_call | solution.py:376
  (2 shorter events, 0.0 us)

commit v2 on v0

v2 whole, which is shorter than its diff:
```python
import math

import jax
import jax.numpy as jnp
from jax import lax
from jax.experimental import pallas as pl
from jax.experimental.pallas import tpu as pltpu
from jax.sharding import PartitionSpec as P

MESH = pl.DeviceIdType.MESH
QH = 32
KVH = 4
HD = 128
T = 160
H = T // 2
SLICE = 1024
CH = 512
NCH = 10
NQ = 8
PER = CH // HD
BLK = 2 * T + 16
AT = ((0, T + 16), (T + 16, T))
IDS = T
NPOS = 17
FIRST = 9
F32 = jnp.float32
BF16 = jnp.bfloat16
FACTOR = math.log2(math.e) / math.sqrt(HD)


def fused_kernel(
    tok, w, scale, cosf, sinf, docs, docs_col,
    out,
    wv, xo, xp, po, p1, sso, rso, ssp, rsp, sx, rx, kp1, kss, krs, ksx, krx, kv, q, acc, top, bias1, bias2,
    w_sem, loc_sem, tok_s, tok_r, sso_s, sso_r, ssp_s, ssp_r, sx_s, sx_r, kss_s, kss_r, ksx_s, ksx_r, h_s, h_r,
):
    dp = lax.axis_index("dp")
    ctx = lax.axis_index("ctx")
    h = dp // 2
    k = dp % 2
    z = ctx // 8
    b = (ctx // 4) % 2
    x = ctx % 4

    def place(h_, k_, z_, b_, x_):
        return (h_ * 2 + k_, z_ * 8 + b_ * 4 + x_)

    sib = place(h, 1 - k, z, b, x)
    par = place(1 - h, k, z, 1 - b, x)
    parx = place(1 - h, 1 - k, z, 1 - b, x)
    z_up = place(h, k, (z + 1) % 8, b, x)
    z_dn = place(h, k, (z + 7) % 8, b, x)
    xi, xm, x2 = (x + 1) % 4, (x + 3) % 4, (x + 2) % 4
    d_i = place(h, k, z, b, xi)
    d_m = place(h, k, z, b, xm)
    d_2 = place(h, k, z, b, x2)
    d_y = place(h, k, z, 1 - b, x)

    def cols(i):
        return pl.ds(pl.multiple_of(((i + 8) % 10) * CH, CH), CH)

    def tok_cols(j):
        return pl.ds(pl.multiple_of(j * SLICE, SLICE), SLICE)

    def w_copy(i):
        return pltpu.make_async_copy(w.at[:, cols(i)], wv.at[i], w_sem.at[i])

    def remote(src, dst, s, r, dev):
        return pltpu.make_async_remote_copy(
            src_ref=src, dst_ref=dst, send_sem=s, recv_sem=r, device_id=dev, device_id_type=MESH
        )

    own_tok = pltpu.make_async_copy(tok.at[:, tok_cols(2 * h + k)], xo.at[pl.ds(0, T)], loc_sem.at[0])
    own_tok.start()
    for i in range(NCH):
        w_copy(i).start()

    bar = pltpu.get_barrier_semaphore()
    for dev in (sib, par, parx, z_dn, d_i, d_m, d_2, d_y):
        pl.semaphore_signal(bar, inc=1, device_id=dev, device_id_type=MESH)
    pl.semaphore_wait(bar, 8)

    def tok_copy(f, far):
        j = 2 * (1 - h) + (1 - k if far else k)
        n = 2 * f + far
        return remote(
            tok.at[pl.ds(f * H, H), tok_cols(j)], xp.at[f, pl.ds(far * H, H)], tok_s.at[n], tok_r.at[n],
            parx if far else par,
        )

    t_sib = remote(tok.at[:, tok_cols(2 * h + 1 - k)], xo.at[pl.ds(T, T)], tok_s.at[4], tok_r.at[4], sib)
    tok_copy(0, 0).start()
    tok_copy(0, 1).start()
    t_sib.start()
    own_tok.wait()
    t_sib.wait_recv()

    def sso_copy(i):
        return remote(sso.at[i], rso.at[i], sso_s.at[i], sso_r.at[i], sib)

    def ssp_copy(i):
        return remote(ssp.at[i], rsp.at[i], ssp_s.at[i], ssp_r.at[i], sib)

    def sx_copy(i):
        return remote(sx.at[i], rx.at[i], sx_s.at[i], sx_r.at[i], par)

    def kss_copy(f):
        return remote(kss.at[f], krs.at[f], kss_s.at[f], kss_r.at[f], sib)

    def ksx_copy(f):
        return remote(ksx.at[f], krx.at[f], ksx_s.at[f], ksx_r.at[f], par)

    def own_part(i, c):
        w_copy(i).wait()
        part = jnp.dot(xo[...], wv[i], preferred_element_type=F32)
        po[i] = part[:T]
        sso[i] = part[T:].astype(BF16)
        sso_copy(i).start()
        return c

    lax.fori_loop(0, 6, own_part, 0)
    for far in range(2):
        tok_copy(0, far).wait_send()
        tok_copy(1, far).start()
    lax.fori_loop(6, NCH, own_part, 0)

    def kv_part(f):
        for far in range(2):
            tok_copy(f, far).wait_recv()
        for i in range(2):
            part = jnp.dot(xp[f], wv[i], preferred_element_type=F32)
            kp1[:, i * CH:(i + 1) * CH] = part[:H]
            kss[f, :, i * CH:(i + 1) * CH] = part[H:].astype(BF16)
        kss_copy(f).start()
        kss_copy(f).wait_recv()
        ksx[f] = (kp1[...] + krs[f].astype(F32)).astype(BF16)
        ksx_copy(f).start()

    def turned(u, rows):
        return u * cosf[rows, :] + pltpu.roll(u, HD // 2, 1) * sinf[rows, :]

    def kv_final(f):
        rows = pl.ds(f * H, H)
        at = AT[f][0]
        ksx_copy(f).wait_recv()
        if f == 0:
            for i in range(2):
                sso_copy(i).wait_recv()
        u = (po[0, rows] + rso[0, rows].astype(F32) + krx[f, :, :CH].astype(F32)) * scale[8]
        for g in range(KVH):
            kv[0, pl.ds(at, H), g * HD:(g + 1) * HD] = turned(u[:, g * HD:(g + 1) * HD], rows).astype(BF16)
        u = (po[1, rows] + rso[1, rows].astype(F32) + krx[f, :, CH:].astype(F32)) * scale[9]
        kv[0, pl.ds(at + H, H), :] = u.astype(BF16)

    def q_part(i, c):
        part = jnp.dot(xp[...].reshape(2 * T, SLICE), wv[i], preferred_element_type=F32)
        p1[i] = jnp.concatenate([part[:H], part[2 * H:3 * H]], axis=0).astype(BF16)
        ssp[i] = jnp.concatenate([part[H:2 * H], part[3 * H:]], axis=0).astype(BF16)
        ssp_copy(i).start()

        @pl.when(i > 2)
        def _():
            q_sum(i - 1)

        return c

    def q_sum(i):
        ssp_copy(i).wait_recv()
        sx[i] = (p1[i].astype(F32) + rsp[i].astype(F32)).astype(BF16)
        sx_copy(i).start()

    def q_parts(lo, hi):
        lax.fori_loop(lo, hi, q_part, 0)

    def q_final(i):
        sso_copy(i).wait_recv()
        sx_copy(i).wait_recv()
        u = (po[i] + rso[i].astype(F32) + rx[i].astype(F32)) * (scale[(i + 8) % 10] * FACTOR)
        for g in range(PER):
            q[i - 2, :, g * HD:(g + 1) * HD] = turned(u[:, g * HD:(g + 1) * HD], pl.ds(0, T)).astype(BF16)

    ya = FIRST + 4 * b
    yb = FIRST + 4 * (1 - b)
    ya_there = FIRST + 4 * (1 - b)
    yb_there = FIRST + 4 * b

    def send(n, f, src, dst, dev):
        at = pl.ds(AT[f][0], AT[f][1])
        return remote(kv.at[src, at], kv.at[dst, at], h_s.at[f, n], h_r.at[f, dst], dev)

    def arrive(f, dst):
        at = pl.ds(AT[f][0], AT[f][1])
        remote(kv.at[dst, at], kv.at[dst, at], h_s.at[f, 0], h_r.at[f, dst], sib).wait_recv()

    row = ((9, xi, 6, d_i), (10, xm, 7, d_m), (11, x2, 8, d_2))

    def near_start(f):
        send(0, f, 0, 1, z_up).start()

        @pl.when(b == 0)
        def _():
            send(12, f, 0, yb_there, d_y).start()

        for n, v, dst, dev in row:
            @pl.when(v > x)
            def _():
                send(n, f, 0, dst, dev).start()

    def plane_start(f):
        arrive(f, 1)
        send(1, f, 1, 2, z_up).start()
        send(2, f, 1, 3, d_i).start()
        send(3, f, 1, 4, d_m).start()
        send(4, f, 1, ya_there, d_y).start()

    def plane_on(f):
        arrive(f, 3)
        if f == 0:
            send(5, f, 3, 5, d_i).start()
        send(6, f, 3, ya_there + 1, d_y).start()
        arrive(f, 4)
        if f == 1:
            send(5, f, 4, 5, d_m).start()
        send(7, f, 4, ya_there + 2, d_y).start()

    def plane_last(f):
        arrive(f, 5)
        send(8, f, 5, ya_there + 3, d_y).start()

    def far_start(f):
        arrive(f, 2)

        @pl.when(b == 1)
        def _():
            send(12, f, 2, yb_there, d_y).start()

        for n, v, dst, dev in row:
            @pl.when(v < x)
            def _():
                send(n, f, 2, dst, dev).start()

    def spread_start(f, which):
        @pl.when(b == which)
        def _():
            arrive(f, yb)
            send(13, f, yb, yb + 1, d_i).start()
            send(14, f, yb, yb + 2, d_m).start()

    def spread_on(f, which):
        @pl.when(b == which)
        def _():
            if f == 0:
                arrive(f, yb + 2)
                send(15, f, yb + 2, yb + 3, d_m).start()
            else:
                arrive(f, yb + 1)
                send(15, f, yb + 1, yb + 3, d_i).start()

    def ya_rest():
        for r in range(4):
            for f in range(2):
                arrive(f, ya + r)

    def yb_rest():
        arrive(0, yb + 1)
        arrive(1, yb + 2)
        for f in range(2):
            arrive(f, yb + 3)

    ydist = 4 - 8 * b
    yo = jnp.where(b == 1, 4, 12)
    away = [jnp.int32(0), jnp.int32(8), jnp.int32(16), 8 + x - xm, 8 + x - xi, 8 + x - x2]
    away += [jnp.where(v < x, x - v, 16 + x - v) for v in (xm, xi, x2)]
    cross_b = [yo + x - v for v in (x, xm, xi, x2)]
    cross_a = [8 - ydist + x - v for v in (x, xm, xi, x2)]
    away += [jnp.where(b == 1, m, n) for m, n in zip(cross_b, cross_a)]
    away += [jnp.where(b == 1, n, m) for m, n in zip(cross_b, cross_a)]

    def make_bias(ref, p0, n):
        mine = docs_col[...].astype(F32)
        col = lax.broadcasted_iota(jnp.int32, (1, n * T), 1).astype(F32)
        seg = jnp.floor((col + 0.5) / H)
        second = seg >= n
        pos = jnp.where(second, seg - n, seg)
        r = col - H * seg + jnp.where(second, float(H), 0.0)
        low = jnp.zeros((T, n * T), F32)
        for i in range(n):
            ids = kv[p0 + i, pl.ds(IDS, 16), :][0:1, 0:T].astype(F32)
            count = jnp.sum((ids < mine).astype(F32), axis=1, keepdims=True)
            count = jnp.where(ctx >= away[p0 + i], count, float(T))
            low = jnp.where(pos == i, count, low)
        keep = r >= low
        if p0 == 0:
            t = lax.broadcasted_iota(jnp.int32, (T, n * T), 0).astype(F32)
            keep = keep & ((pos > 0.0) | (r <= t))
        ref[...] = jnp.where(keep, 0.0, -jnp.inf)

    def attend(i, p0, n, bias, last):
        g = i // 2
        lanes = pl.ds(pl.multiple_of(g * HD, HD), HD)
        where = pl.ds(p0, n)

        def rows(lo):
            parts = [kv[where, pl.ds(AT[f][0] + lo, H), lanes].reshape(n * H, HD) for f in range(2)]
            return jnp.concatenate(parts, axis=0)

        keys = rows(0)
        vals = jnp.concatenate([rows(H), jnp.ones((n * T, HD), BF16)], axis=1)
        for j in range(PER):
            qj = q[i, :, j * HD:(j + 1) * HD]
            s = lax.dot_general(qj, keys, (((1,), (1,)), ((), ())), preferred_element_type=F32) + bias[...]
            m = jnp.max(s, axis=1, keepdims=True)
            if p0 > 0:
                before = top[i, j]
                m = jnp.maximum(before, m)
                p = jnp.exp2(s - m[:, :1])
            else:
                p = jnp.exp2(s - m)
            o = jnp.dot(p.astype(BF16), vals, preferred_element_type=F32)
            if p0 > 0:
                fade = jnp.exp2(before - m)
                o = o + acc[i, j] * jnp.concatenate([fade, fade], axis=1)
            if last:
                out[i, :, j * HD:(j + 1) * HD] = (o[:, :HD] / o[:, HD:]).astype(BF16)
            else:
                acc[i, j] = o
                top[i, j] = jnp.broadcast_to(m, (T, HD))

    kv[0, pl.ds(IDS, 16), :] = jnp.zeros((16, CH), BF16)
    kv[0, pl.ds(IDS, 16), pl.ds(0, T)] = jnp.broadcast_to(docs[...].astype(F32), (16, T)).astype(BF16)
    kv_part(0)
    kv_final(0)
    near_start(0)
    kv_part(1)
    q_parts(2, 4)
    plane_start(0)
    q_parts(4, 6)
    kv_final(1)
    near_start(1)
    spread_start(0, 1)
    plane_on(0)
    q_parts(6, 8)
    far_start(0)
    plane_start(1)
    q_parts(8, 10)
    q_sum(9)
    spread_start(1, 1)
    spread_on(0, 1)
    plane_last(0)
    plane_on(1)
    spread_start(0, 0)
    far_start(1)
    spread_on(0, 0)
    spread_on(1, 1)
    plane_last(1)
    spread_start(1, 0)
    for f in range(2):
        for dst in (6, 7, 8):
            arrive(f, dst)
    make_bias(bias1, 0, 9)
    spread_on(1, 0)

    def first(i, c):
        q_final(i + 2)
        attend(i, 0, 9, bias1, False)
        return c

    lax.fori_loop(0, NQ, first, 0)

    @pl.when(b == 1)
    def _():
        yb_rest()

    @pl.when(b == 0)
    def _():
        ya_rest()

    make_bias(bias2, 9, 4)

    def second(i, c):
        attend(i, 9, 4, bias2, False)
        return c

    lax.fori_loop(0, NQ, second, 0)

    @pl.when(b == 0)
    def _():
        yb_rest()

    @pl.when(b == 1)
    def _():
        ya_rest()

    make_bias(bias2, 13, 4)

    def third(i, c):
        attend(i, 13, 4, bias2, True)
        return c

    lax.fori_loop(0, NQ, third, 0)

    for f in range(2):
        for far in range(2):
            if f == 1:
                tok_copy(f, far).wait_send()
        kss_copy(f).wait_send()
        ksx_copy(f).wait_send()
        for n in range(16):
            send(n, f, 0, 1, z_up).wait_send()
    t_sib.wait_send()

    def sent(i, c):
        sso_copy(i).wait_send()

        @pl.when(i > 1)
        def _():
            ssp_copy(i).wait_send()
            sx_copy(i).wait_send()

        return c

    lax.fori_loop(0, NCH, sent, 0)


def fused(tok, w, scale, cosf, sinf, docs, docs_col):
    vmem = pl.BlockSpec(memory_space=pltpu.VMEM)
    hbm = pl.BlockSpec(memory_space=pl.ANY)
    chunks = pltpu.VMEM((NCH, T, CH), BF16)
    half = pltpu.VMEM((2, H, 2 * CH), BF16)
    dma = pltpu.SemaphoreType.DMA
    return pl.pallas_call(
        fused_kernel,
        out_shape=jax.ShapeDtypeStruct((NQ, T, CH), BF16),
        in_specs=[hbm, hbm, vmem, vmem, vmem, vmem, vmem],
        out_specs=vmem,
        scratch_shapes=[
            pltpu.VMEM((NCH, SLICE, CH), BF16),
            pltpu.VMEM((2 * T, SLICE), BF16),
            pltpu.VMEM((2, T, SLICE), BF16),
            pltpu.VMEM((NCH, T, CH), F32),
            chunks, chunks, chunks, chunks, chunks, chunks, chunks,
            pltpu.VMEM((H, 2 * CH), F32),
            half, half, half, half,
            pltpu.VMEM((NPOS, BLK, CH), BF16),
            pltpu.VMEM((NQ, T, CH), BF16),
            pltpu.VMEM((NQ, PER, T, 2 * HD), F32),
            pltpu.VMEM((NQ, PER, T, HD), F32),
            pltpu.VMEM((T, FIRST * T), F32),
            pltpu.VMEM((T, 4 * T), F32),
            dma((NCH,)), dma((1,)), dma((5,)), dma((5,)),
            dma((NCH,)), dma((NCH,)), dma((NCH,)), dma((NCH,)), dma((NCH,)), dma((NCH,)),
            dma((2,)), dma((2,)), dma((2,)), dma((2,)),
            dma((2, 16)), dma((2, NPOS)),
        ],
        compiler_params=pltpu.CompilerParams(
            collective_id=0, has_side_effects=True, vmem_limit_bytes=60 << 20
        ),
        name="fused",
    )(tok, w, scale, cosf, sinf, docs, docs_col)


def local(tokens, w_qkv, col_scale, doc_ids):
    positions = lax.axis_index("ctx") * T + jnp.arange(T, dtype=jnp.int32)
    half = HD // 2
    freqs = jnp.exp(-math.log(500000.0) * 2.0 * jnp.arange(half, dtype=F32) / HD)
    angles = positions.astype(F32)[:, None] * freqs[None, :]
    cosine, sine = jnp.cos(angles), jnp.sin(angles)
    cosf = jnp.concatenate([cosine, cosine], axis=1)
    sinf = jnp.concatenate([-sine, sine], axis=1)
    out = fused(
        tokens[0], w_qkv, col_scale.reshape(NCH, 1, CH), cosf, sinf, doc_ids, doc_ids.reshape(T, 1)
    )
    return out.transpose(1, 0, 2).reshape(1, T, QH * HD)


def solution(mesh):
    return jax.shard_map(
        local,
        mesh=mesh,
        in_specs=(P("dp", "ctx", None), P("dp", None), P(), P("dp", "ctx")),
        out_specs=P("dp", "ctx", None),
        check_vma=False,
    )
```

time: 548 us -> 120 us (0.22)
  the two profiles are of different devices: /device:TPU:72 before, /device:TPU:16 now
where the time goes in v2:
time: 120 us
  Pallas kernels  114 us (95%)
  local copies, waits for them, and re-layouts  4.93 us (4%)
    pallas_call x1, Pallas kernels, fused(): pl.pallas_call(fused_kernel, out_shape=jax.ShapeDtypeStruct((NQ, T, CH),...  114 us

profile of v2, /device:TPU:16, one launch (start us, length us, event | category | flops | bytes accessed | tf_op | source)
XLA Modules:
  0.0 120.0 jit_solution(8358072309519981894)
XLA Ops:
  0.0 1.4 %copy.5.docs_col = s32[160,1]{1,0:T(8,128)} copy(s32[160,1]{0,1:T(1,128)} %bitcast.7) | data formatting | bytes 1280 | tf_op jit(solution)/shard_map/reshape | solution.py:471
  1.4 0.4 fusion
  1.8 0.8 pad_maximum_fusion
  2.6 113.9 %fused.1 = bf16[8,160,512]{2,1,0:T(8,128)(2,1)} custom-call(bf16[160,4096]{1,0:T(8,128)(2,1)} %bitcast.5, bf16[1024,5120]{1,0:T(8,128)(2,1)} %w.1, f32[10,1,512]{2,1,0:T(1,128)} %bitcast.6, f32[160,128]{1,0:T(8,128)} %get-tuple-element.8.cosf, f32[160,128]{1,0:T(8,128)} %get-tuple-element.9.sinf, s32[1,160]{1,0:T(1,128)} %docs.1, s32[160,1]{1,0:T(8,128)} %copy.5.docs_col), custom_call_target="tpu_custom_call" | custom-call | tf_op jit(solution)/shard_map/fused/pallas_call | solution.py:431
  116.4 2.0 %copy.6 = bf16[160,8,512]{2,1,0:T(8,128)(2,1)S(1)} copy(bf16[160,8,512]{2,0,1:T(8,128)(2,1)} %bitcast.4) | data formatting | bytes 2621440 | tf_op jit(solution)/shard_map/transpose | solution.py:473
  118.5 1.5 %reshape.21 = bf16[1,160,4096]{2,1,0:T(8,128)(2,1)} reshape(bf16[160,8,512]{2,1,0:T(8,128)(2,1)S(1)} %copy.6) | data formatting | bytes 2621440 | tf_op jit(solution)/shard_map/reshape | solution.py:473
  (2 shorter events, 0.0 us)

commit v3 on v2

--- a/solution.py
+++ b/solution.py
@@ -16,22 +16,24 @@
 SLICE = 1024
 CH = 512
 NCH = 10
-NQ = 8
 PER = CH // HD
+GROUP = QH // KVH
+WIDE = GROUP * T
 BLK = 2 * T + 16
 AT = ((0, T + 16), (T + 16, T))
 IDS = T
 NPOS = 17
 FIRST = 9
+UNROLL = 4
 F32 = jnp.float32
 BF16 = jnp.bfloat16
 FACTOR = math.log2(math.e) / math.sqrt(HD)
 
 
 def fused_kernel(
-    tok, w, scale, cosf, sinf, docs, docs_col,
+    tok, w, scale, docs,
     out,
-    wv, xo, xp, po, p1, sso, rso, ssp, rsp, sx, rx, kp1, kss, krs, ksx, krx, kv, q, acc, top, bias1, bias2,
+    wv, xo, xp, po, p1, sso, rso, ssp, rsp, sx, rx, kp1, kss, krs, ksx, krx, kv, q, acc, top, tot, drow, low, cosf, sinf,
     w_sem, loc_sem, tok_s, tok_r, sso_s, sso_r, ssp_s, ssp_r, sx_s, sx_r, kss_s, kss_r, ksx_s, ksx_r, h_s, h_r,
 ):
     dp = lax.axis_index("dp")
@@ -146,10 +148,10 @@
         if f == 0:
             for i in range(2):
                 sso_copy(i).wait_recv()
-        u = (po[0, rows] + rso[0, rows].astype(F32) + krx[f, :, :CH].astype(F32)) * scale[8]
+        u = (po[0, rows] + rso[0, rows].astype(F32) + krx[f, :, :CH].astype(F32)) * scale[:, 8 * CH:9 * CH]
         for g in range(KVH):
             kv[0, pl.ds(at, H), g * HD:(g + 1) * HD] = turned(u[:, g * HD:(g + 1) * HD], rows).astype(BF16)
-        u = (po[1, rows] + rso[1, rows].astype(F32) + krx[f, :, CH:].astype(F32)) * scale[9]
+        u = (po[1, rows] + rso[1, rows].astype(F32) + krx[f, :, CH:].astype(F32)) * scale[:, 9 * CH:]
         kv[0, pl.ds(at + H, H), :] = u.astype(BF16)
 
     def q_part(i, c):
@@ -175,14 +177,13 @@
     def q_final(i):
         sso_copy(i).wait_recv()
         sx_copy(i).wait_recv()
-        u = (po[i] + rso[i].astype(F32) + rx[i].astype(F32)) * (scale[(i + 8) % 10] * FACTOR)
-        for g in range(PER):
-            q[i - 2, :, g * HD:(g + 1) * HD] = turned(u[:, g * HD:(g + 1) * HD], pl.ds(0, T)).astype(BF16)
-
-    ya = FIRST + 4 * b
-    yb = FIRST + 4 * (1 - b)
-    ya_there = FIRST + 4 * (1 - b)
-    yb_there = FIRST + 4 * b
+        u = (po[i] + rso[i].astype(F32) + rx[i].astype(F32)) * (scale[:, cols(i)] * FACTOR)
+        heads = [turned(u[:, g * HD:(g + 1) * HD], pl.ds(0, T)) for g in range(PER)]
+        at = pl.ds(pl.multiple_of((i % 2) * PER * T, PER * T), PER * T)
+        q[i // 2 - 1, :, at] = jnp.concatenate(heads, axis=0).T.astype(BF16)
+
+    yb = FIRST
+    ya = FIRST + 4
 
     def send(n, f, src, dst, dev):
         at = pl.ds(AT[f][0], AT[f][1])
@@ -199,7 +200,7 @@
 
         @pl.when(b == 0)
         def _():
-            send(12, f, 0, yb_there, d_y).start()
+            send(12, f, 0, yb, d_y).start()
 
         for n, v, dst, dev in row:
             @pl.when(v > x)
@@ -211,28 +212,32 @@
         send(1, f, 1, 2, z_up).start()
         send(2, f, 1, 3, d_i).start()
         send(3, f, 1, 4, d_m).start()
-        send(4, f, 1, ya_there, d_y).start()
 
     def plane_on(f):
         arrive(f, 3)
         if f == 0:
             send(5, f, 3, 5, d_i).start()
-        send(6, f, 3, ya_there + 1, d_y).start()
         arrive(f, 4)
         if f == 1:
             send(5, f, 4, 5, d_m).start()
-        send(7, f, 4, ya_there + 2, d_y).start()
-
-    def plane_last(f):
+
+    def cross(f):
+        send(4, f, 1, ya, d_y).start()
+
+    def cross_on(f):
+        send(6, f, 3, ya + 1, d_y).start()
+        send(7, f, 4, ya + 2, d_y).start()
+
+    def cross_last(f):
         arrive(f, 5)
-        send(8, f, 5, ya_there + 3, d_y).start()
+        send(8, f, 5, ya + 3, d_y).start()
 
     def far_start(f):
         arrive(f, 2)
 
         @pl.when(b == 1)
         def _():
-            send(12, f, 2, yb_there, d_y).start()
+            send(12, f, 2, yb, d_y).start()
 
         for n, v, dst, dev in row:
             @pl.when(v < x)
@@ -273,30 +278,32 @@
     away += [jnp.where(v < x, x - v, 16 + x - v) for v in (xm, xi, x2)]
     cross_b = [yo + x - v for v in (x, xm, xi, x2)]
     cross_a = [8 - ydist + x - v for v in (x, xm, xi, x2)]
-    away += [jnp.where(b == 1, m, n) for m, n in zip(cross_b, cross_a)]
-    away += [jnp.where(b == 1, n, m) for m, n in zip(cross_b, cross_a)]
-
-    def make_bias(ref, p0, n):
-        mine = docs_col[...].astype(F32)
-        col = lax.broadcasted_iota(jnp.int32, (1, n * T), 1).astype(F32)
-        seg = jnp.floor((col + 0.5) / H)
-        second = seg >= n
-        pos = jnp.where(second, seg - n, seg)
-        r = col - H * seg + jnp.where(second, float(H), 0.0)
-        low = jnp.zeros((T, n * T), F32)
-        for i in range(n):
-            ids = kv[p0 + i, pl.ds(IDS, 16), :][0:1, 0:T].astype(F32)
-            count = jnp.sum((ids < mine).astype(F32), axis=1, keepdims=True)
-            count = jnp.where(ctx >= away[p0 + i], count, float(T))
-            low = jnp.where(pos == i, count, low)
-        keep = r >= low
-        if p0 == 0:
-            t = lax.broadcasted_iota(jnp.int32, (T, n * T), 0).astype(F32)
-            keep = keep & ((pos > 0.0) | (r <= t))
-        ref[...] = jnp.where(keep, 0.0, -jnp.inf)
-
-    def attend(i, p0, n, bias, last):
-        g = i // 2
+    away += cross_b + cross_a
+
+    def prepare():
+        kv[0, pl.ds(IDS, 16), :] = jnp.zeros((16, CH), BF16)
+        kv[0, pl.ds(IDS, 16), pl.ds(0, T)] = jnp.broadcast_to(docs[...].astype(F32), (16, T)).astype(BF16)
+        for j in range(GROUP):
+            drow[:, j * T:(j + 1) * T] = docs[...].astype(F32)
+        lane = lax.broadcasted_iota(jnp.int32, (T, HD), 1)
+        i = jnp.where(lane < HD // 2, lane, lane - HD // 2).astype(F32)
+        freq = jnp.exp(-math.log(500000.0) * 2.0 * i / HD)
+        pos = ctx * T + lax.broadcasted_iota(jnp.int32, (T, HD), 0)
+        angle = pos.astype(F32) * freq
+        cosf[...] = jnp.cos(angle)
+        sine = jnp.sin(angle)
+        sinf[...] = jnp.where(lane < HD // 2, -sine, sine)
+
+    def make_low(p0, n):
+        doc = lax.broadcasted_iota(jnp.int32, (8, 1), 0).astype(F32)
+        mine = (drow[...] == doc).astype(F32)
+        for p in range(p0, p0 + n):
+            ids = kv[p, pl.ds(IDS, 16), :][0:1, 0:T].astype(F32)
+            count = jnp.sum((ids < doc).astype(F32), axis=1, keepdims=True)
+            count = jnp.where(ctx >= away[p], count, float(T))
+            low[p] = jnp.sum(mine * count, axis=0, keepdims=True)
+
+    def attend(g, p0, n, last):
         lanes = pl.ds(pl.multiple_of(g * HD, HD), HD)
         where = pl.ds(p0, n)
 
@@ -304,100 +311,104 @@
             parts = [kv[where, pl.ds(AT[f][0] + lo, H), lanes].reshape(n * H, HD) for f in range(2)]
             return jnp.concatenate(parts, axis=0)
 
-        keys = rows(0)
-        vals = jnp.concatenate([rows(H), jnp.ones((n * T, HD), BF16)], axis=1)
-        for j in range(PER):
-            qj = q[i, :, j * HD:(j + 1) * HD]
-            s = lax.dot_general(qj, keys, (((1,), (1,)), ((), ())), preferred_element_type=F32) + bias[...]
-            m = jnp.max(s, axis=1, keepdims=True)
-            if p0 > 0:
-                before = top[i, j]
-                m = jnp.maximum(before, m)
-                p = jnp.exp2(s - m[:, :1])
-            else:
-                p = jnp.exp2(s - m)
-            o = jnp.dot(p.astype(BF16), vals, preferred_element_type=F32)
-            if p0 > 0:
-                fade = jnp.exp2(before - m)
-                o = o + acc[i, j] * jnp.concatenate([fade, fade], axis=1)
-            if last:
-                out[i, :, j * HD:(j + 1) * HD] = (o[:, :HD] / o[:, HD:]).astype(BF16)
-            else:
-                acc[i, j] = o
-                top[i, j] = jnp.broadcast_to(m, (T, HD))
-
-    kv[0, pl.ds(IDS, 16), :] = jnp.zeros((16, CH), BF16)
-    kv[0, pl.ds(IDS, 16), pl.ds(0, T)] = jnp.broadcast_to(docs[...].astype(F32), (16, T)).astype(BF16)
+        s = jnp.dot(rows(0), q[g], preferred_element_type=F32)
+        r = lax.broadcasted_iota(jnp.int32, (H, WIDE), 0).astype(F32)
+        parts = []
+        for f in range(2):
+            for i in range(n):
+                keep = r >= low[p0 + i] - f * H
+                if p0 + i == 0:
+                    t = lax.broadcasted_iota(jnp.int32, (1, WIDE), 1).astype(F32)
+                    t = t - T * jnp.floor((t + 0.5) / T)
+                    keep = keep & (r <= t - f * H)
+                at = (f * n + i) * H
+                parts.append(jnp.where(keep, s[at:at + H], -jnp.inf))
+        s = jnp.concatenate(parts, axis=0)
+        m = jnp.max(s, axis=0, keepdims=True)
+        if p0 > 0:
+            before = top[g, 0:1]
+            m = jnp.maximum(before, m)
+        p = jnp.exp2(s - m)
+        total = jnp.sum(p, axis=0, keepdims=True)
+        o = lax.dot_general(rows(H), p.astype(BF16), (((0,), (0,)), ((), ())), preferred_element_type=F32)
+        if p0 > 0:
+            fade = jnp.exp2(before - m)
+            o = o + acc[g] * fade
+            total = total + tot[g, 0:1] * fade
+        if last:
+            o = (o / total).T.astype(BF16)
+            for j in range(GROUP):
+                at = pl.multiple_of((g * GROUP + j) * HD, HD)
+                out[:, pl.ds(at, HD)] = o[j * T:(j + 1) * T]
+        else:
+            acc[g] = o
+            top[g] = jnp.broadcast_to(m, (8, WIDE))
+            tot[g] = jnp.broadcast_to(total, (8, WIDE))
+
     kv_part(0)
+    prepare()
     kv_final(0)
     near_start(0)
     kv_part(1)
     q_parts(2, 4)
     plane_start(0)
+    cross(0)
     q_parts(4, 6)
     kv_final(1)
     near_start(1)
     spread_start(0, 1)
     plane_on(0)
+    far_start(0)
+    cross_on(0)
     q_parts(6, 8)
-    far_start(0)
     plane_start(1)
+    spread_start(1, 1)
     q_parts(8, 10)
     q_sum(9)
-    spread_start(1, 1)
     spread_on(0, 1)
-    plane_last(0)
+    cross_last(0)
+    spread_start(0, 0)
     plane_on(1)
-    spread_start(0, 0)
     far_start(1)
+    cross(1)
+    cross_on(1)
     spread_on(0, 0)
     spread_on(1, 1)
-    plane_last(1)
+    cross_last(1)
+
+    def first(g, c):
+        q_final(2 * g + 2)
+        q_final(2 * g + 3)
+        attend(g, 0, 6, False)
+        return c
+
+    make_low(0, 6)
+    lax.fori_loop(0, 1, first, 0)
     spread_start(1, 0)
+    lax.fori_loop(1, 2, first, 0)
+    spread_on(1, 0)
+    lax.fori_loop(2, KVH, first, 0)
     for f in range(2):
         for dst in (6, 7, 8):
             arrive(f, dst)
-    make_bias(bias1, 0, 9)
-    spread_on(1, 0)
-
-    def first(i, c):
-        q_final(i + 2)
-        attend(i, 0, 9, bias1, False)
-        return c
-
-    lax.fori_loop(0, NQ, first, 0)
-
-    @pl.when(b == 1)
-    def _():
-        yb_rest()
-
-    @pl.when(b == 0)
-    def _():
-        ya_rest()
-
-    make_bias(bias2, 9, 4)
-
-    def second(i, c):
-        attend(i, 9, 4, bias2, False)
-        return c
-
-    lax.fori_loop(0, NQ, second, 0)
-
-    @pl.when(b == 0)
-    def _():
-        yb_rest()
-
-    @pl.when(b == 1)
-    def _():
-        ya_rest()
-
-    make_bias(bias2, 13, 4)
-
-    def third(i, c):
-        attend(i, 13, 4, bias2, True)
-        return c
-
-    lax.fori_loop(0, NQ, third, 0)
+
+    yb_rest()
+    make_low(6, 7)
+
+    def second(g, c):
+        attend(g, 6, 7, False)
+        return c
+
+    lax.fori_loop(0, KVH, second, 0, unroll=UNROLL)
+
+    ya_rest()
+    make_low(13, 4)
+
+    def third(g, c):
+        attend(g, 13, 4, True)
+        return c
+
+    lax.fori_loop(0, KVH, third, 0, unroll=UNROLL)
 
     for f in range(2):
         for far in range(2):
@@ -422,7 +433,7 @@
     lax.fori_loop(0, NCH, sent, 0)
 
 
-def fused(tok, w, scale, cosf, sinf, docs, docs_col):
+def fused(tok, w, scale, docs):
     vmem = pl.BlockSpec(memory_space=pltpu.VMEM)
     hbm = pl.BlockSpec(memory_space=pl.ANY)
     chunks = pltpu.VMEM((NCH, T, CH), BF16)
@@ -430,8 +441,8 @@
     dma = pltpu.SemaphoreType.DMA
     return pl.pallas_call(
         fused_kernel,
-        out_shape=jax.ShapeDtypeStruct((NQ, T, CH), BF16),
-        in_specs=[hbm, hbm, vmem, vmem, vmem, vmem, vmem],
+        out_shape=jax.ShapeDtypeStruct((T, QH * HD), BF16),
+        in_specs=[hbm, hbm, vmem, vmem],
         out_specs=vmem,
         scratch_shapes=[
             pltpu.VMEM((NCH, SLICE, CH), BF16),
@@ -442,11 +453,14 @@
             pltpu.VMEM((H, 2 * CH), F32),
             half, half, half, half,
             pltpu.VMEM((NPOS, BLK, CH), BF16),
-            pltpu.VMEM((NQ, T, CH), BF16),
-            pltpu.VMEM((NQ, PER, T, 2 * HD), F32),
-            pltpu.VMEM((NQ, PER, T, HD), F32),
-            pltpu.VMEM((T, FIRST * T), F32),
-            pltpu.VMEM((T, 4 * T), F32),
+            pltpu.VMEM((KVH, HD, WIDE), BF16),
+            pltpu.VMEM((KVH, HD, WIDE), F32),
+            pltpu.VMEM((KVH, 8, WIDE), F32),
+            pltpu.VMEM((KVH, 8, WIDE), F32),
+            pltpu.VMEM((1, WIDE), F32),
+            pltpu.VMEM((NPOS, 1, WIDE), F32),
+            pltpu.VMEM((T, HD), F32),
+            pltpu.VMEM((T, HD), F32),
             dma((NCH,)), dma((1,)), dma((5,)), dma((5,)),
             dma((NCH,)), dma((NCH,)), dma((NCH,)), dma((NCH,)), dma((NCH,)), dma((NCH,)),
             dma((2,)), dma((2,)), dma((2,)), dma((2,)),
@@ -456,21 +470,11 @@
             collective_id=0, has_side_effects=True, vmem_limit_bytes=60 << 20
         ),
         name="fused",
-    )(tok, w, scale, cosf, sinf, docs, docs_col)
+    )(tok, w, scale, docs)
 
 
 def local(tokens, w_qkv, col_scale, doc_ids):
-    positions = lax.axis_index("ctx") * T + jnp.arange(T, dtype=jnp.int32)
-    half = HD // 2
-    freqs = jnp.exp(-math.log(500000.0) * 2.0 * jnp.arange(half, dtype=F32) / HD)
-    angles = positions.astype(F32)[:, None] * freqs[None, :]
-    cosine, sine = jnp.cos(angles), jnp.sin(angles)
-    cosf = jnp.concatenate([cosine, cosine], axis=1)
-    sinf = jnp.concatenate([-sine, sine], axis=1)
-    out = fused(
-        tokens[0], w_qkv, col_scale.reshape(NCH, 1, CH), cosf, sinf, doc_ids, doc_ids.reshape(T, 1)
-    )
-    return out.transpose(1, 0, 2).reshape(1, T, QH * HD)
+    return fused(tokens[0], w_qkv, col_scale.reshape(1, -1), doc_ids)[None]
 
 
 def solution(mesh):

time: 120 us -> 97.3 us (0.81)
  Pallas kernels: 114 us -> 93.6 us
  local copies, waits for them, and re-layouts: 4.93 us -> 2.49 us
    pallas_call x1, Pallas kernels: 114 us -> 93.6 us  [fused(): pl.pallas_call(fused_kernel, out_shape=jax.ShapeDtypeStruct((T, QH * HD),...]
    reshape x2 -> x0, local copies, waits for them, and re-layouts: 2.89 us -> none  [the longest x1 1.47 us: local(): return out.transpose(1, 0, 2).reshape(1, T, QH * HD)]
    unnamed x0 -> x1, local copies, waits for them, and re-layouts: none -> 2.49 us
    transpose x1 -> x0, local copies, waits for them, and re-layouts: 2.04 us -> none  [local(): return out.transpose(1, 0, 2).reshape(1, T, QH * HD)]
where the time goes in v3:
time: 97.3 us; the launch traced here: 96.1 us
  Pallas kernels  93.6 us (96%)
  local copies, waits for them, and re-layouts  2.49 us (3%)
    pallas_call x1, Pallas kernels, fused(): pl.pallas_call(fused_kernel, out_shape=jax.ShapeDtypeStruct((T, QH * HD),...  93.6 us
    unnamed x1, local copies, waits for them, and re-layouts  2.49 us

profile of v3, /device:TPU:16, one launch (start us, length us, event | category | flops | bytes accessed | tf_op | source)
XLA Modules:
  0.0 96.1 jit_solution(5453858391908149842)
XLA Ops:
  0.0 93.6 %fused.1 = bf16[160,4096]{1,0:T(8,128)(2,1)} custom-call(bf16[160,4096]{1,0:T(8,128)(2,1)} %bitcast.4, bf16[1024,5120]{1,0:T(8,128)(2,1)} %w.1, f32[1,5120]{1,0:T(1,128)} %bitcast.5, s32[1,160]{1,0:T(1,128)} %docs.1), custom_call_target="tpu_custom_call" | custom-call | tf_op jit(solution)/shard_map/fused/pallas_call | solution.py:442
  93.6 2.5 %copy.6 = bf16[1,160,4096]{2,1,0:T(8,128)(2,1)} copy(bf16[1,160,4096]{2,1,0:T(8,128)(2,1)} %bitcast.3) | data formatting | bytes 2621440

commit v4 on v3

--- a/solution.py
+++ b/solution.py
@@ -179,7 +179,7 @@
         sx_copy(i).wait_recv()
         u = (po[i] + rso[i].astype(F32) + rx[i].astype(F32)) * (scale[:, cols(i)] * FACTOR)
         heads = [turned(u[:, g * HD:(g + 1) * HD], pl.ds(0, T)) for g in range(PER)]
-        at = pl.ds(pl.multiple_of((i % 2) * PER * T, PER * T), PER * T)
+        at = pl.ds((i % 2) * PER * T, PER * T)
         q[i // 2 - 1, :, at] = jnp.concatenate(heads, axis=0).T.astype(BF16)
 
     yb = FIRST
@@ -304,7 +304,7 @@
             low[p] = jnp.sum(mine * count, axis=0, keepdims=True)
 
     def attend(g, p0, n, last):
-        lanes = pl.ds(pl.multiple_of(g * HD, HD), HD)
+        lanes = pl.ds(g * HD if isinstance(g, int) else pl.multiple_of(g * HD, HD), HD)
         where = pl.ds(p0, n)
 
         def rows(lo):
@@ -367,36 +367,40 @@
     q_sum(9)
     spread_on(0, 1)
     cross_last(0)
+    q_final(2)
     spread_start(0, 0)
     plane_on(1)
+    q_final(3)
     far_start(1)
     cross(1)
     cross_on(1)
+    q_final(4)
     spread_on(0, 0)
     spread_on(1, 1)
     cross_last(1)
-
-    def first(g, c):
-        q_final(2 * g + 2)
-        q_final(2 * g + 3)
-        attend(g, 0, 6, False)
-        return c
-
+    q_final(5)
     make_low(0, 6)
-    lax.fori_loop(0, 1, first, 0)
+    attend(0, 0, 6, False)
     spread_start(1, 0)
-    lax.fori_loop(1, 2, first, 0)
+    attend(1, 0, 6, False)
+    q_final(6)
     spread_on(1, 0)
-    lax.fori_loop(2, KVH, first, 0)
+    q_final(7)
     for f in range(2):
         for dst in (6, 7, 8):
             arrive(f, dst)
-
+    make_low(6, 3)
+    attend(2, 0, 9, False)
+    attend(0, 6, 3, False)
+    attend(1, 6, 3, False)
+    q_final(8)
+    q_final(9)
+    attend(3, 0, 9, False)
     yb_rest()
-    make_low(6, 7)
+    make_low(9, 4)
 
     def second(g, c):
-        attend(g, 6, 7, False)
+        attend(g, 9, 4, False)
         return c
 
     lax.fori_loop(0, KVH, second, 0, unroll=UNROLL)
@@ -441,7 +445,7 @@
     dma = pltpu.SemaphoreType.DMA
     return pl.pallas_call(
         fused_kernel,
-        out_shape=jax.ShapeDtypeStruct((T, QH * HD), BF16),
+        out_shape=pltpu.VMEM((T, QH * HD), BF16),
         in_specs=[hbm, hbm, vmem, vmem],
         out_specs=vmem,
         scratch_shapes=[
@@ -467,7 +471,7 @@
             dma((2, 16)), dma((2, NPOS)),
         ],
         compiler_params=pltpu.CompilerParams(
-            collective_id=0, has_side_effects=True, vmem_limit_bytes=60 << 20
+            collective_id=0, has_side_effects=True, vmem_limit_bytes=57 << 20
         ),
         name="fused",
     )(tok, w, scale, docs)

time: 97.3 us -> 94.7 us (0.973)
  Pallas kernels: 93.6 us -> 91.9 us
  local copies, waits for them, and re-layouts: 2.49 us -> 1.06 us
    pallas_call x1, Pallas kernels: 93.6 us -> 91.9 us  [fused(): pl.pallas_call(fused_kernel, out_shape=pltpu.VMEM((T, QH * HD), BF16), in...]
    unnamed x1, local copies, waits for them, and re-layouts: 2.49 us -> 1.06 us
where the time goes in v4:
time: 94.7 us; the launch traced here: 93 us
  Pallas kernels  91.9 us (97%)
  local copies, waits for them, and re-layouts  1.06 us (1%)
    pallas_call x1, Pallas kernels, fused(): pl.pallas_call(fused_kernel, out_shape=pltpu.VMEM((T, QH * HD), BF16), in...  91.9 us

profile of v4, /device:TPU:16, one launch (start us, length us, event | category | flops | bytes accessed | tf_op | source)
XLA Modules:
  0.0 93.0 jit_solution(733121429265903589)
XLA Ops:
  0.0 91.9 %fused.1 = bf16[160,4096]{1,0:T(8,128)(2,1)S(1)} custom-call(bf16[160,4096]{1,0:T(8,128)(2,1)} %bitcast.4, bf16[1024,5120]{1,0:T(8,128)(2,1)} %w.1, f32[1,5120]{1,0:T(1,128)} %bitcast.5, s32[1,160]{1,0:T(1,128)} %docs.1), custom_call_target="tpu_custom_call" | custom-call | tf_op jit(solution)/shard_map/fused/pallas_call | solution.py:446
  91.9 1.1 %copy.6 = bf16[1,160,4096]{2,1,0:T(8,128)(2,1)} copy(bf16[1,160,4096]{2,1,0:T(8,128)(2,1)S(1)} %bitcast.3) | data formatting | bytes 2621440
